TPU v7x, 256 devices: a whole 4x4x8 slice. The times are simulated.
256 devices in a mesh: dp: 2 (over z_hi), context: 32 (over y, x, core), tensor: 4 (over z_lo).
Axes of the slice: x: 4, y: 4, z: 8 (z_hi: 2, z_lo: 4; z = z_hi * 4 + z_lo), core: 2. Of those that a mesh axis runs over, the one named last changes fastest.
Arguments:
- value_in: bfloat16 [2, 16384, 2048], P('dp', 'context', 'tensor'), may hold values from -7 to 7
- key_in: bfloat16 [2, 16384, 2048], P('dp', 'context', 'tensor'), may hold values from -7 to 7
- query_in: bfloat16 [2, 16384, 2048], P('dp', 'context', 'tensor'), may hold values from -7 to 7
- filter_taps: bfloat16 [16384, 2048], P('context', 'tensor'), may hold values from -8 to 8
- out_weight: bfloat16 [2048, 2048], P('tensor'), may hold values from -0.125 to 0.125
- cotangent: bfloat16 [2, 16384, 2048], P('dp', 'context', 'tensor'), may hold values from -7 to 7
Outputs:
- mixed_out: bfloat16 [2, 16384, 2048], P('dp', 'context', 'tensor')
- grad_value: bfloat16 [2, 16384, 2048], P('dp', 'context', 'tensor')
- grad_key: bfloat16 [2, 16384, 2048], P('dp', 'context', 'tensor')
- grad_query: bfloat16 [2, 16384, 2048], P('dp', 'context', 'tensor')
- grad_filter: float32 [16384, 2048], P('context', 'tensor')
All inputs are finite; a program needn't handle non-finite values.
Results may differ from a plain program's by a relative error of at most 0.015.
Values may be sent and summed in bfloat16 or wider, within the bound.
No kernel may reach another device: no remote copies, remote signals or barrier semaphores. Data moves between devices by JAX's collectives and lax.ppermute only.
A program may use at most 128 MiB of HBM per device.

v0:
```python
import math

import jax
import jax.numpy as jnp
from jax import lax
from jax.sharding import PartitionSpec as P


def unit_wave(first_index, second_index, period):
    phase_angle = (first_index * second_index % period).astype(jnp.float32) * (
        -2.0 * math.pi / period
    )
    return (jnp.cos(phase_angle), jnp.sin(phase_angle))


def spectral_tables(row_count, block_size):
    radix_size = 2 * row_count
    radix_cos, radix_sin = unit_wave(
        jnp.arange(row_count, dtype=jnp.int32)[:, None],
        jnp.arange(radix_size, dtype=jnp.int32)[None, :],
        radix_size,
    )
    radix_cos = radix_cos.astype(jnp.bfloat16)
    radix_sin = radix_sin.astype(jnp.bfloat16)
    radix_fwd = jnp.stack([radix_cos, radix_sin], 0)
    radix_inv = jnp.stack([radix_cos.T, radix_sin.T], 0)
    block_cos, block_sin = unit_wave(
        jnp.arange(block_size, dtype=jnp.int32)[:, None],
        jnp.arange(block_size, dtype=jnp.int32)[None, :],
        block_size,
    )
    block_cos = block_cos.astype(jnp.bfloat16)
    block_sin = block_sin.astype(jnp.bfloat16)
    block_fwd = jnp.stack(
        [jnp.stack([block_cos, block_sin], 1), jnp.stack([-block_sin, block_cos], 1)], 0
    )
    block_inv = jnp.stack(
        [jnp.stack([block_cos, -block_sin], 1), jnp.stack([block_sin, block_cos], 1)], 0
    )
    return (radix_fwd, radix_inv, block_fwd, block_inv)


def product(left_side, right_side, conjugate):
    left_re = left_side[..., 0, :, :, :]
    left_im = left_side[..., 1, :, :, :]
    if conjugate:
        left_im = -left_im
    right_re = right_side[..., 0, :, :, :]
    right_im = right_side[..., 1, :, :, :]
    joined = jnp.stack(
        [left_re * right_re - left_im * right_im, left_re * right_im + left_im * right_re], -4
    )
    return joined.astype(jnp.bfloat16)


def forward_transform(signal_in, tables, twiddle, to_columns, to_rows):
    item_count, block_size, chan_count = signal_in.shape
    row_count = tables[0].shape[1]
    gathered = to_columns(
        signal_in.reshape(item_count, row_count, block_size // row_count, chan_count)
    )
    first_section = jnp.einsum(
        "odk,mdjc->mokjc", tables[0], gathered, preferred_element_type=jnp.float32
    )
    turned_re = first_section[:, 0] * twiddle[0] - first_section[:, 1] * twiddle[1]
    turned_im = first_section[:, 0] * twiddle[1] + first_section[:, 1] * twiddle[0]
    turned = jnp.stack([turned_re, turned_im], 1).astype(jnp.bfloat16)
    regrouped = to_rows(turned)
    return jnp.einsum("rjoq,mrkjc->mokqc", tables[2], regrouped, preferred_element_type=jnp.float32)


def inverse_transform(spectrum_in, tables, twiddle, to_rows, to_columns, points):
    back_section = jnp.einsum(
        "rqoj,mrkqc->mokjc", tables[3], spectrum_in, preferred_element_type=jnp.float32
    )
    unturned_re = back_section[:, 0] * twiddle[0] + back_section[:, 1] * twiddle[1]
    unturned_im = back_section[:, 1] * twiddle[0] - back_section[:, 0] * twiddle[1]
    unturned = jnp.stack([unturned_re, unturned_im], 1).astype(jnp.bfloat16)
    regrouped = to_rows(unturned)
    grid_out = jnp.einsum(
        "rkd,mrkjc->mdjc", tables[1], regrouped, preferred_element_type=jnp.float32
    ) * (1.0 / points)
    returned = to_columns(grid_out.astype(jnp.bfloat16))
    return returned.reshape(returned.shape[0], -1, returned.shape[-1])


def shards(value_in, key_in, query_in, filter_taps, out_weight, cotangent):
    seq_count, block_size, chan_count = value_in.shape
    row_count = lax.axis_size("context")
    position = lax.axis_index("context")
    radix_size = 2 * row_count
    points = radix_size * block_size
    part_size = block_size // row_count
    tables = spectral_tables(row_count, block_size)
    local_cols = position * part_size + jnp.arange(part_size, dtype=jnp.int32)
    fwd_cos, fwd_sin = unit_wave(
        jnp.arange(radix_size, dtype=jnp.int32)[:, None], local_cols[None, :], points
    )
    twiddle_fwd = (fwd_cos[:, :, None], fwd_sin[:, :, None])
    local_freqs = 2 * position + jnp.arange(2, dtype=jnp.int32)
    back_cos, back_sin = unit_wave(
        local_freqs[:, None], jnp.arange(block_size, dtype=jnp.int32)[None, :], points
    )
    twiddle_back = (back_cos[:, :, None], back_sin[:, :, None])
    gated = (key_in.astype(jnp.float32) * value_in.astype(jnp.float32)).astype(jnp.bfloat16)
    d_gate = cotangent.astype(jnp.float32)
    d_conv = (d_gate * query_in.astype(jnp.float32)).astype(jnp.bfloat16)
    taps = filter_taps[None]
    spectra = forward_transform(
        jnp.concatenate([gated, taps], 0),
        tables,
        twiddle_fwd,
        lambda piece_in: lax.all_to_all(
            piece_in, "context", split_axis=1, concat_axis=1, tiled=True
        ),
        lambda piece_in: lax.all_to_all(
            piece_in, "context", split_axis=2, concat_axis=3, tiled=True
        ),
    )
    spec_gated = spectra[:seq_count]
    spec_taps = spectra[seq_count:]
    conv = inverse_transform(
        product(spec_gated, spec_taps, False),
        tables,
        twiddle_back,
        lambda piece_in: lax.all_to_all(
            piece_in, "context", split_axis=3, concat_axis=2, tiled=True
        ),
        lambda piece_in: lax.all_to_all(
            piece_in, "context", split_axis=1, concat_axis=1, tiled=True
        ),
        points,
    )
    spec_dconv = forward_transform(
        d_conv,
        tables,
        twiddle_fwd,
        lambda piece_in: lax.all_to_all(
            piece_in, "context", split_axis=1, concat_axis=1, tiled=True
        ),
        lambda piece_in: lax.all_to_all(
            piece_in, "context", split_axis=2, concat_axis=3, tiled=True
        ),
    )
    stacked = jnp.concatenate(
        [product(spec_taps, spec_dconv, True), product(spec_gated, spec_dconv, True)], 0
    )
    signals = inverse_transform(
        stacked,
        tables,
        twiddle_back,
        lambda piece_in: lax.all_to_all(
            piece_in, "context", split_axis=3, concat_axis=2, tiled=True
        ),
        lambda piece_in: lax.all_to_all(
            piece_in, "context", split_axis=1, concat_axis=1, tiled=True
        ),
        points,
    )
    grad_gated = signals[:seq_count]
    filter_terms = signals[seq_count:]
    gate_out = (query_in.astype(jnp.float32) * conv.astype(jnp.float32)).astype(jnp.bfloat16)
    partial_out = jnp.einsum(
        "stc,co->sto", gate_out, out_weight, preferred_element_type=jnp.float32
    )
    mixed_out = lax.psum_scatter(
        partial_out.astype(jnp.bfloat16), "tensor", scatter_dimension=2, tiled=True
    )
    grad_query = (d_gate * conv.astype(jnp.float32)).astype(jnp.bfloat16)
    grad_value = (grad_gated.astype(jnp.float32) * key_in.astype(jnp.float32)).astype(jnp.bfloat16)
    grad_key = (grad_gated.astype(jnp.float32) * value_in.astype(jnp.float32)).astype(jnp.bfloat16)
    loss_scale = 1.0 / math.sqrt(lax.axis_size("dp") * seq_count * row_count * block_size)
    filter_local = jnp.sum(filter_terms.astype(jnp.float32), 0)
    grad_filter = lax.psum(filter_local.astype(jnp.bfloat16), "dp").astype(jnp.float32) * loss_scale
    return (mixed_out, grad_value, grad_key, grad_query, grad_filter)


def solution(mesh):
    return jax.shard_map(
        shards,
        mesh=mesh,
        in_specs=(
            P("dp", "context", "tensor"),
            P("dp", "context", "tensor"),
            P("dp", "context", "tensor"),
            P("context", "tensor"),
            P("tensor", None),
            P("dp", "context", "tensor"),
        ),
        out_specs=(
            P("dp", "context", "tensor"),
            P("dp", "context", "tensor"),
            P("dp", "context", "tensor"),
            P("dp", "context", "tensor"),
            P("context", "tensor"),
        ),
        check_vma=False,
    )
```

profile of v0, /device:TPU:1, one launch (start us, length us, event | category | flops | bytes accessed | tf_op | source)
XLA Modules:
  0.0 383.9 jit_solution(5660266174322176433)
XLA Ops:
  8.0 2.3 fusion.45
  10.3 8.6 %all-to-all-start.4 = ((bf16[1,32,16,512]{3,2,0,1:T(8,128)(2,1)}), bf16[1,32,16,512]{3,2,0,1:T(8,128)(2,1)}, u32[]{:S(2)}, u32[]{:S(2)}) async-start(bf16[1,32,16,512]{3,2,0,1:T(8,128)(2,1)} %bitcast.258), calls=%async_computation.5 | async-start | bytes 1048576 | tf_op jit(solution)/shard_map/all_to_all | solution.py:138
  21.3 9.2 %all-to-all-done.4 = bf16[1,32,16,512]{3,2,0,1:T(8,128)(2,1)} async-done(((bf16[1,32,16,512]{3,2,0,1:T(8,128)(2,1)}), bf16[1,32,16,512]{3,2,0,1:T(8,128)(2,1)}, u32[]{:S(2)}, u32[]{:S(2)}) %all-to-all-start.4) | async-done | bytes 524320 | tf_op jit(solution)/shard_map/all_to_all | solution.py:138
  30.6 4.0 %all-to-all-start = ((bf16[2,32,16,512]{3,2,0,1:T(8,128)(2,1)}), bf16[2,32,16,512]{3,2,0,1:T(8,128)(2,1)S(1)}, u32[]{:S(2)}, u32[]{:S(2)}) async-start(bf16[2,32,16,512]{3,2,0,1:T(8,128)(2,1)} %copy.99), calls=%async_computation | async-start | bytes 2097152 | tf_op jit(solution)/shard_map/all_to_all | solution.py:113
  34.8 1.8 convolution_bitcast_fusion.2
  37.5 3.5 copy.120
  41.0 10.9 %all-to-all-done = bf16[2,32,16,512]{3,2,0,1:T(8,128)(2,1)S(1)} async-done(((bf16[2,32,16,512]{3,2,0,1:T(8,128)(2,1)}), bf16[2,32,16,512]{3,2,0,1:T(8,128)(2,1)S(1)}, u32[]{:S(2)}, u32[]{:S(2)}) %all-to-all-start) | async-done | bytes 1048608 | tf_op jit(solution)/shard_map/all_to_all | solution.py:113
  51.9 5.4 %all-to-all-start.5 = ((bf16[1,2,64,16,512]{4,1,3,0,2:T(2,128)(2,1)}), bf16[1,2,64,16,512]{4,1,3,0,2:T(2,128)(2,1)}, u32[]{:S(2)}, u32[]{:S(2)}) async-start(bf16[1,2,64,16,512]{4,1,3,0,2:T(2,128)(2,1)} %copy.120), calls=%async_computation.6 | async-start | bytes 4194304 | tf_op jit(solution)/shard_map/all_to_all | solution.py:141
  60.3 6.3 %copy.101 = bf16[2,2,64,16,512]{4,1,3,0,2:T(2,128)(2,1)} copy(bf16[2,2,64,16,512]{4,2,1,3,0:T(8,128)(2,1)S(1)} %pad_maximum_fusion) | data formatting | bytes 8388608 | tf_op jit(solution)/shard_map/stack | solution.py:67
  66.7 18.4 %all-to-all-done.5 = bf16[1,2,64,16,512]{4,1,3,0,2:T(2,128)(2,1)} async-done(((bf16[1,2,64,16,512]{4,1,3,0,2:T(2,128)(2,1)}), bf16[1,2,64,16,512]{4,1,3,0,2:T(2,128)(2,1)}, u32[]{:S(2)}, u32[]{:S(2)}) %all-to-all-start.5) | async-done | bytes 2097184 | tf_op jit(solution)/shard_map/all_to_all | solution.py:141
  85.1 7.2 %all-to-all-start.1 = ((bf16[2,2,64,16,512]{4,1,3,0,2:T(2,128)(2,1)}), bf16[2,2,64,16,512]{4,1,3,0,2:T(2,128)(2,1)}, u32[]{:S(2)}, u32[]{:S(2)}) async-start(bf16[2,2,64,16,512]{4,1,3,0,2:T(2,128)(2,1)} %copy.101), calls=%async_computation.1 | async-start | bytes 8388608 | tf_op jit(solution)/shard_map/all_to_all | solution.py:116
  92.3 4.0 %fusion.64 = bf16[512,1,512]{2,0,1:T(8,128)(2,1)S(1)} fusion(), kind=kLoop, calls=%fused_computation.109 | loop fusion | flops 4718592 | bytes 524288 | tf_op jit(solution)/shard_map/neg | solution.py:35
  96.3 4.3 %sine_convert_fusion = (bf16[512,1,512]{2,0,1:T(8,128)(2,1)S(1)}, bf16[512,1,512]{2,0,1:T(8,128)(2,1)S(1)}) fusion(), kind=kLoop, calls=%fused_computation.101 | loop fusion | flops 4194304 | bytes 1048576 | tf_op jit(solution)/shard_map/convert_element_type | solution.py:33
  100.6 1.6 fusion.43
  102.4 2.3 copy.121
  104.9 4.4 %convolution_bitcast_fusion.1 = f32[1,2,2,512,512]{3,4,1,2,0:T(8,128)} fusion(bf16[2,2,512,512,1]{3,2,1,0,4:T(8,128)(2,1)S(1)} %bitcast.259, bf16[1,512,2,512]{3,1,0,2:T(8,128)(2,1)S(1)} %get-tuple-element.22, bf16[1,512,2,512]{3,1,0,2:T(8,128)(2,1)S(1)} %get-tuple-element.27), kind=kOutput, calls=%fused_computation.22 | convolution fusion | flops 2151677952 | bytes 8388608 | tf_op jit(solution)/shard_map/rjoq,mrkjc->mokqc/dot_general | solution.py:69
  109.3 33.1 %all-to-all-done.1 = bf16[2,2,64,16,512]{4,1,3,0,2:T(2,128)(2,1)} async-done(((bf16[2,2,64,16,512]{4,1,3,0,2:T(2,128)(2,1)}), bf16[2,2,64,16,512]{4,1,3,0,2:T(2,128)(2,1)}, u32[]{:S(2)}, u32[]{:S(2)}) %all-to-all-start.1) | async-done | bytes 4194336 | tf_op jit(solution)/shard_map/all_to_all | solution.py:116
  142.4 3.2 copy.102
  146.8 4.6 %fusion.11 = f32[2,2,2,512,512]{3,4,1,2,0:T(8,128)S(1)} fusion(bf16[2,2,2,512,512,1]{4,3,2,1,0,5:T(8,128)(2,1)S(1)} %bitcast.257, bf16[1,512,2,512]{3,1,0,2:T(8,128)(2,1)S(1)} %get-tuple-element.22, bf16[1,512,2,512]{3,1,0,2:T(8,128)(2,1)S(1)} %copy-done.9), kind=kOutput, calls=%fused_computation.17 | convolution fusion | flops 4299161600 | bytes 14680064 | tf_op jit(solution)/shard_map/rjoq,mrkjc->mokqc/dot_general | solution.py:69
  151.4 2.8 fusion.25
  154.2 1.8 fusion.55
  156.0 4.5 %fusion.14 = f32[2,2,2,512,512]{3,4,1,2,0:T(8,128)S(1)} fusion(bf16[1,1,2,512,512]{3,4,1,2,0:T(8,128)(2,1)S(1)} %get-tuple-element.6, bf16[1,1,2,512,512]{3,4,1,2,0:T(8,128)(2,1)S(1)} %get-tuple-element.7, bf16[1,1,2,512,512]{3,4,1,2,0:T(8,128)(2,1)S(1)} %get-tuple-element.5, bf16[1,1,2,512,512]{3,4,1,2,0:T(8,128)(2,1)S(1)} %get-tuple-element.12, ...), kind=kOutput, calls=%fused_computation.18 | convolution fusion | flops 4315938816 | bytes 14680064 | tf_op jit(solution)/shard_map/rqoj,mrkqc->mokjc/dot_general | solution.py:73
  161.9 2.3 pad_maximum_fusion.1
  164.2 11.3 %copy.133 = bf16[2,2,2,512,512]{4,1,2,0,3:T(2,128)(2,1)} copy(bf16[2,2,2,512,512]{3,4,1,2,0:T(8,128)(2,1)} %pad_maximum_fusion.1) | data formatting | bytes 8388608 | tf_op jit(solution)/shard_map/stack | solution.py:78
  175.5 8.0 %all-to-all-start.6 = ((bf16[2,2,2,512,512]{4,1,2,0,3:T(2,128)(2,1)}), bf16[2,2,2,512,512]{4,1,2,0,3:T(2,128)(2,1)}, u32[]{:S(2)}, u32[]{:S(2)}) async-start(bf16[2,2,2,512,512]{4,1,2,0,3:T(2,128)(2,1)} %copy.133), calls=%async_computation.7 | async-start | bytes 8388608 | tf_op jit(solution)/shard_map/all_to_all | solution.py:152
  183.5 4.2 %convolution_bitcast_fusion.3 = f32[1,2,2,512,512]{3,4,1,2,0:T(8,128)S(1)} fusion(bf16[1,512,2,512]{3,1,2,0:T(8,128)(2,1)} %get-tuple-element.28, bf16[1,512,2,512]{3,1,2,0:T(8,128)(2,1)} %get-tuple-element.21, bf16[1,2,512,512]{2,3,1,0:T(8,128)(2,1)} %get-tuple-element.14, bf16[1,2,512,512]{2,3,1,0:T(8,128)(2,1)S(1)} %get-tuple-element.13), kind=kOutput, calls=%fused_computation.24 | convolution fusion | flops 2149580800 | bytes 8388608 | tf_op jit(solution)/shard_map/rqoj,mrkqc->mokjc/dot_general | solution.py:73
  188.4 1.6 pad_maximum_fusion.4
  190.0 6.2 %copy.113 = bf16[1,2,2,512,512]{4,1,2,0,3:T(2,128)(2,1)} copy(bf16[1,2,2,512,512]{3,4,1,2,0:T(8,128)(2,1)} %pad_maximum_fusion.4) | data formatting | bytes 4194304 | tf_op jit(solution)/shard_map/stack | solution.py:78
  196.1 37.8 %all-to-all-done.6 = bf16[2,2,2,512,512]{4,1,2,0,3:T(2,128)(2,1)} async-done(((bf16[2,2,2,512,512]{4,1,2,0,3:T(2,128)(2,1)}), bf16[2,2,2,512,512]{4,1,2,0,3:T(2,128)(2,1)}, u32[]{:S(2)}, u32[]{:S(2)}) %all-to-all-start.6) | async-done | bytes 4194336 | tf_op jit(solution)/shard_map/all_to_all | solution.py:152
  233.9 8.3 %all-to-all-start.2 = ((bf16[1,2,2,512,512]{4,1,2,0,3:T(2,128)(2,1)}), bf16[1,2,2,512,512]{4,1,2,0,3:T(2,128)(2,1)}, u32[]{:S(2)}, u32[]{:S(2)}) async-start(bf16[1,2,2,512,512]{4,1,2,0,3:T(2,128)(2,1)} %copy.113), calls=%async_computation.2 | async-start | bytes 4194304 | tf_op jit(solution)/shard_map/all_to_all | solution.py:126
  242.3 3.6 copy.134
  245.9 6.3 %copy.135 = bf16[2,2,32,2,16,512]{5,3,2,1,4,0:T(2,128)(2,1)} copy(bf16[2,2,32,2,16,512]{5,4,2,3,1,0:T(8,128)(2,1)S(1)} %bitcast.253) | data formatting | bytes 8388608 | tf_op jit(solution)/shard_map/all_to_all | solution.py:152
  252.2 7.2 %all_to_all.76 = bf16[2,2,64,16,512]{4,2,1,3,0:T(8,128)(2,1)} reshape(bf16[2,2,32,2,16,512]{5,3,2,1,4,0:T(2,128)(2,1)} %copy.135) | data formatting | bytes 8388608 | tf_op jit(solution)/shard_map/all_to_all | solution.py:152
  259.4 2.9 fusion.36
  263.9 6.1 %all-to-all-done.2 = bf16[1,2,2,512,512]{4,1,2,0,3:T(2,128)(2,1)} async-done(((bf16[1,2,2,512,512]{4,1,2,0,3:T(2,128)(2,1)}), bf16[1,2,2,512,512]{4,1,2,0,3:T(2,128)(2,1)}, u32[]{:S(2)}, u32[]{:S(2)}) %all-to-all-start.2) | async-done | bytes 2097184 | tf_op jit(solution)/shard_map/all_to_all | solution.py:126
  270.0 6.0 %all-to-all-start.7 = ((bf16[2,32,16,512]{3,2,0,1:T(8,128)(2,1)}), bf16[2,32,16,512]{3,2,0,1:T(8,128)(2,1)S(1)}, u32[]{:S(2)}, u32[]{:S(2)}) async-start(bf16[2,32,16,512]{3,2,0,1:T(8,128)(2,1)} %copy.136), calls=%async_computation.8 | async-start | bytes 2097152 | tf_op jit(solution)/shard_map/all_to_all | solution.py:155
  276.0 2.0 copy.114
  278.0 3.5 copy.115
  281.5 4.1 %reshape.594 = bf16[2,64,16,512]{3,1,0,2:T(8,128)(2,1)} reshape(bf16[1,2,32,2,16,512]{5,3,2,1,4,0:T(2,128)(2,1)} %copy.115) | data formatting | bytes 4194304 | tf_op jit(solution)/shard_map/reshape.10
  285.6 2.0 fusion.39
  288.8 4.5 %all-to-all-done.7 = bf16[2,32,16,512]{3,2,0,1:T(8,128)(2,1)S(1)} async-done(((bf16[2,32,16,512]{3,2,0,1:T(8,128)(2,1)}), bf16[2,32,16,512]{3,2,0,1:T(8,128)(2,1)S(1)}, u32[]{:S(2)}, u32[]{:S(2)}) %all-to-all-start.7) | async-done | bytes 1048608 | tf_op jit(solution)/shard_map/all_to_all | solution.py:155
  293.3 4.6 %all-to-all-start.3 = ((bf16[1,32,16,512]{3,2,0,1:T(8,128)(2,1)}), bf16[1,32,16,512]{3,2,0,1:T(8,128)(2,1)}, u32[]{:S(2)}, u32[]{:S(2)}) async-start(bf16[1,32,16,512]{3,2,0,1:T(8,128)(2,1)} %copy.116), calls=%async_computation.3 | async-start | bytes 1048576 | tf_op jit(solution)/shard_map/all_to_all | solution.py:129
  299.1 10.5 %all-to-all-done.3 = bf16[1,32,16,512]{3,2,0,1:T(8,128)(2,1)} async-done(((bf16[1,32,16,512]{3,2,0,1:T(8,128)(2,1)}), bf16[1,32,16,512]{3,2,0,1:T(8,128)(2,1)}, u32[]{:S(2)}, u32[]{:S(2)}) %all-to-all-start.3) | async-done | bytes 524320 | tf_op jit(solution)/shard_map/all_to_all | solution.py:129
  309.6 3.8 fusion.17
  314.5 2.0 fusion.49
  316.4 2.4 fusion.47
  318.8 54.2 %all-reduce.2.cloned.1.call-done = bf16[512,512]{1,0:T(8,128)(2,1)} async-done(((bf16[512,512]{1,0:T(8,128)(2,1)}), bf16[512,512]{1,0:T(8,128)(2,1)}) %all-reduce.2.cloned.1.call-update) | async-done | bytes 524304 | tf_op jit(solution)/shard_map/psum | solution.py:174
  373.1 2.2 convert_multiply_fusion.6
  (46 shorter events, 15.7 us)
Async XLA Ops:
  8.0 301.6 %copy-start = (bf16[512,2048]{1,0:T(8,128)(2,1)S(1)}, bf16[512,2048]{1,0:T(8,128)(2,1)}, u32[]{:S(2)}) copy-start(bf16[512,2048]{1,0:T(8,128)(2,1)} %param.10) | copy-start | bytes 6291460
  8.0 11.0 %copy-start.3 = (bf16[1,512,512]{2,1,0:T(8,128)(2,1)S(1)}, bf16[1,512,512]{2,1,0:T(8,128)(2,1)}, u32[]{:S(2)}) copy-start(bf16[1,512,512]{2,1,0:T(8,128)(2,1)} %param.6) | copy-start | bytes 1572868
  8.0 11.0 %copy-start.5 = (bf16[1,512,512]{2,1,0:T(8,128)(2,1)S(1)}, bf16[1,512,512]{2,1,0:T(8,128)(2,1)}, u32[]{:S(2)}) copy-start(bf16[1,512,512]{2,1,0:T(8,128)(2,1)} %param.7) | copy-start | bytes 1572868
  10.3 20.3 %all-to-all-start.4 = ((bf16[1,32,16,512]{3,2,0,1:T(8,128)(2,1)}), bf16[1,32,16,512]{3,2,0,1:T(8,128)(2,1)}, u32[]{:S(2)}, u32[]{:S(2)}) async-start(bf16[1,32,16,512]{3,2,0,1:T(8,128)(2,1)} %bitcast.258), calls=%async_computation.5 | async-start | bytes 1048576 | tf_op jit(solution)/shard_map/all_to_all | solution.py:138
  30.6 21.3 %all-to-all-start = ((bf16[2,32,16,512]{3,2,0,1:T(8,128)(2,1)}), bf16[2,32,16,512]{3,2,0,1:T(8,128)(2,1)S(1)}, u32[]{:S(2)}, u32[]{:S(2)}) async-start(bf16[2,32,16,512]{3,2,0,1:T(8,128)(2,1)} %copy.99), calls=%async_computation | async-start | bytes 2097152 | tf_op jit(solution)/shard_map/all_to_all | solution.py:113
  51.9 33.2 %all-to-all-start.5 = ((bf16[1,2,64,16,512]{4,1,3,0,2:T(2,128)(2,1)}), bf16[1,2,64,16,512]{4,1,3,0,2:T(2,128)(2,1)}, u32[]{:S(2)}, u32[]{:S(2)}) async-start(bf16[1,2,64,16,512]{4,1,3,0,2:T(2,128)(2,1)} %copy.120), calls=%async_computation.6 | async-start | bytes 4194304 | tf_op jit(solution)/shard_map/all_to_all | solution.py:141
  85.1 57.3 %all-to-all-start.1 = ((bf16[2,2,64,16,512]{4,1,3,0,2:T(2,128)(2,1)}), bf16[2,2,64,16,512]{4,1,3,0,2:T(2,128)(2,1)}, u32[]{:S(2)}, u32[]{:S(2)}) async-start(bf16[2,2,64,16,512]{4,1,3,0,2:T(2,128)(2,1)} %copy.101), calls=%async_computation.1 | async-start | bytes 8388608 | tf_op jit(solution)/shard_map/all_to_all | solution.py:116
  102.2 2.7 copy-start.8
  145.6 1.2 copy-start.9
  146.8 4.6 %copy-start.1 = (f32[1,2,2,512,512]{3,4,1,2,0:T(8,128)S(1)}, f32[1,2,2,512,512]{3,4,1,2,0:T(8,128)}, u32[]{:S(2)}) copy-start(f32[1,2,2,512,512]{3,4,1,2,0:T(8,128)} %convolution_bitcast_fusion.1) | copy-start | bytes 12582916
  154.2 1.8 copy-start.6
  154.2 1.8 copy-start.7
  175.5 58.4 %all-to-all-start.6 = ((bf16[2,2,2,512,512]{4,1,2,0,3:T(2,128)(2,1)}), bf16[2,2,2,512,512]{4,1,2,0,3:T(2,128)(2,1)}, u32[]{:S(2)}, u32[]{:S(2)}) async-start(bf16[2,2,2,512,512]{4,1,2,0,3:T(2,128)(2,1)} %copy.133), calls=%async_computation.7 | async-start | bytes 8388608 | tf_op jit(solution)/shard_map/all_to_all | solution.py:152
  233.9 36.1 %all-to-all-start.2 = ((bf16[1,2,2,512,512]{4,1,2,0,3:T(2,128)(2,1)}), bf16[1,2,2,512,512]{4,1,2,0,3:T(2,128)(2,1)}, u32[]{:S(2)}, u32[]{:S(2)}) async-start(bf16[1,2,2,512,512]{4,1,2,0,3:T(2,128)(2,1)} %copy.113), calls=%async_computation.2 | async-start | bytes 4194304 | tf_op jit(solution)/shard_map/all_to_all | solution.py:126
  270.0 23.3 %all-to-all-start.7 = ((bf16[2,32,16,512]{3,2,0,1:T(8,128)(2,1)}), bf16[2,32,16,512]{3,2,0,1:T(8,128)(2,1)S(1)}, u32[]{:S(2)}, u32[]{:S(2)}) async-start(bf16[2,32,16,512]{3,2,0,1:T(8,128)(2,1)} %copy.136), calls=%async_computation.8 | async-start | bytes 2097152 | tf_op jit(solution)/shard_map/all_to_all | solution.py:155
  293.3 16.3 %all-to-all-start.3 = ((bf16[1,32,16,512]{3,2,0,1:T(8,128)(2,1)}), bf16[1,32,16,512]{3,2,0,1:T(8,128)(2,1)}, u32[]{:S(2)}, u32[]{:S(2)}) async-start(bf16[1,32,16,512]{3,2,0,1:T(8,128)(2,1)} %copy.116), calls=%async_computation.3 | async-start | bytes 1048576 | tf_op jit(solution)/shard_map/all_to_all | solution.py:129
  297.9 75.2 %all-reduce.2.cloned.1.call-start = ((), (), s32[]{:S(2)}) async-start(), calls=%async_computation.10 | async-start | bytes 1048576 | tf_op jit(solution)/shard_map/psum | solution.py:174
  299.0 77.0 %reduce-scatter.2.cloned.1.call-start = ((), (), s32[]{:S(2)}) async-start(), calls=%async_computation.9 | async-start | bytes 2621440 | tf_op jit(solution)/shard_map/reduce_scatter | solution.py:166
  313.4 1.0 copy-start.2
  313.4 3.0 copy-start.4
Sparse Core Ops, SparseCore 0:
  302.1 70.9 all-reduce.1
Sparse Core Ops, SparseCore 1:
  313.5 62.4 reduce-scatter.1
where the time goes:
time: 390 us; the launch traced here: 384 us
  waiting for transfers between devices  186 us (48%)
  local copies, waits for them, and re-layouts  66.8 us (17%)
  starting transfers between devices  52.2 us (13%)
  other arithmetic  33.3 us (9%)
  matrix products  29.7 us (8%)
  between operations  16.3 us (4%)
    psum x1, waiting for transfers between devices, shards(): lax.psum(filter_local.astype(jnp.bfloat16), 'dp').astype(jnp.float32)  54.2 us
    all_to_all x2, waiting for transfers between devices, shards(): lax.all_to_all(piece_in, 'context', split_axis=2, concat_axis=3, tiled=True)  51.5 us
    all_to_all x2, waiting for transfers between devices, shards(): lax.all_to_all(piece_in, 'context', split_axis=3, concat_axis=2, tiled=True)  43.9 us
    all_to_all x4, waiting for transfers between devices, shards(): lax.all_to_all(piece_in, 'context', split_axis=1, concat_axis=1, tiled=True)  35.1 us
    all_to_all x4, starting transfers between devices, shards(): lax.all_to_all(piece_in, 'context', split_axis=1, concat_axis=1, tiled=True)  23.2 us
    all_to_all x5, local copies, waits for them, and re-layouts, shards(): lax.all_to_all(piece_in, 'context', split_axis=3, concat_axis=2, tiled=True)  22.7 us
    another operation x2, local copies, waits for them, and re-layouts, inverse_transform(): unturned = jnp.stack([unturned_re, unturned_im], 1).astype(jnp.bfloat16)  17.5 us
    all_to_all x2, starting transfers between devices, shards(): lax.all_to_all(piece_in, 'context', split_axis=3, concat_axis=2, tiled=True)  16.3 us
  transfers between devices with their start and end apart: 10, of which 10 were waited for; matrix products, arithmetic and copies ran while one was open for 22% of the time, Pallas kernels for 0%

commit v1 on v0

v1 whole, which is shorter than its diff:
```python
import functools
import math

import jax
import jax.numpy as jnp
import numpy as np
from jax import lax
from jax.experimental import pallas as pl
from jax.experimental.pallas import tpu as pltpu
from jax.sharding import PartitionSpec as P

LANES = 128
F32 = jnp.float32
BF16 = jnp.bfloat16


def right_angle_tables(source_count, length):
    radix = length // LANES
    quarters = radix // source_count
    row = np.arange(radix)
    slow = (row % source_count) * quarters + row // source_count
    freq = np.arange(radix) + 0.25
    slow_angle = -2.0 * np.pi * freq[:, None] * slow[None, :] / radix
    slow_fwd = np.concatenate([np.cos(slow_angle), np.sin(slow_angle)], 0)
    slow_inv = slow_fwd.T
    fast = np.arange(LANES)
    turn_angle = -2.0 * np.pi * freq[:, None] * fast[None, :] / length
    turn_cos, turn_sin = np.cos(turn_angle), np.sin(turn_angle)
    fast_angle = -2.0 * np.pi * ((fast[:, None] * fast[None, :]) % LANES) / LANES
    fast_cos, fast_sin = np.cos(fast_angle), np.sin(fast_angle)
    fast_fwd = np.block([[fast_cos, fast_sin], [-fast_sin, fast_cos]])
    fast_inv = np.block([[fast_cos, -fast_sin], [fast_sin, fast_cos]])
    turn = np.stack([turn_cos, turn_sin, turn_cos / length, turn_sin / length])
    return (
        jnp.asarray(slow_fwd, BF16),
        jnp.asarray(fast_fwd, BF16),
        jnp.asarray(fast_inv, BF16),
        jnp.asarray(slow_inv, BF16),
        jnp.asarray(turn, F32),
    )


def dot(left, right):
    return jnp.dot(left, right, preferred_element_type=F32)


def flip(square):
    extent = square.shape[1]
    rows = lax.broadcasted_iota(jnp.int32, (extent, extent), 0)
    cols = lax.broadcasted_iota(jnp.int32, (extent, extent), 1)
    unit = jnp.where(rows == cols, 1.0, 0.0).astype(BF16)
    turned = lax.dot_general(unit, square, (((1,), (1,)), ((), ())), preferred_element_type=F32)
    return turned.astype(BF16)


def times(left, right):
    return (left.astype(F32) * right.astype(F32)).astype(BF16)


def gate_kernel(value_ref, key_ref, query_ref, cot_ref, taps_ref, out_ref):
    group = out_ref.shape[1] // 3
    signals = (
        times(key_ref[...], value_ref[...]),
        taps_ref[...],
        times(cot_ref[...], query_ref[...]),
    )
    for slot, signal in enumerate(signals):
        turned = flip(signal)
        out_ref[:, slot * group : (slot + 1) * group, :] = turned.reshape(
            out_ref.shape[0], group, turned.shape[1]
        )


def spread(in_ref, first_row, wide_ref, group):
    for source in range(in_ref.shape[0]):
        rows = in_ref[source, first_row : first_row + group, :].astype(F32)
        for quarter in range(wide_ref.shape[0]):
            wide_ref[quarter, source * group : (source + 1) * group, :] = rows[
                :, quarter * LANES : (quarter + 1) * LANES
            ]


def forward_pair(wide_ref, chan, group, tables):
    slow_fwd, fast_fwd, _, _, turn = tables
    quarters, rows, _ = wide_ref.shape
    columns = [
        jnp.concatenate(
            [wide_ref[q, pl.ds(one, rows // group, stride=group), :] for q in range(quarters)], 0
        )
        for one in (chan, chan + 1)
    ]
    first = dot(slow_fwd[...], jnp.concatenate(columns, 1).astype(BF16))
    radix = first.shape[0] // 2
    turn_cos, turn_sin = turn[0], turn[1]
    sides = []
    for side in range(2):
        lanes = slice(side * LANES, (side + 1) * LANES)
        part_re, part_im = first[:radix, lanes], first[radix:, lanes]
        sides.append(
            jnp.concatenate(
                [
                    (part_re * turn_cos - part_im * turn_sin).astype(BF16),
                    (part_re * turn_sin + part_im * turn_cos).astype(BF16),
                ],
                1,
            )
        )
    return dot(jnp.concatenate(sides, 0), fast_fwd[...])


def product(left, right, conjugate):
    left_re, left_im = left[:, :LANES], left[:, LANES:]
    right_re, right_im = right[:, :LANES], right[:, LANES:]
    if conjugate:
        both_re = left_re * right_re + left_im * right_im
        both_im = left_re * right_im - left_im * right_re
    else:
        both_re = left_re * right_re - left_im * right_im
        both_im = left_re * right_im + left_im * right_re
    return jnp.concatenate([both_re, both_im], 1).astype(BF16)


def inverse_pair(spectrum, chan, wide_ref, group, tables):
    _, _, fast_inv, slow_inv, turn = tables
    back = dot(spectrum, fast_inv[...])
    radix = back.shape[0] // 2
    turn_cos, turn_sin = turn[2], turn[3]
    parts_re, parts_im = [], []
    for side in range(2):
        rows = slice(side * radix, (side + 1) * radix)
        back_re, back_im = back[rows, :LANES], back[rows, LANES:]
        parts_re.append((back_re * turn_cos + back_im * turn_sin).astype(BF16))
        parts_im.append((back_im * turn_cos - back_re * turn_sin).astype(BF16))
    unturned = jnp.concatenate(
        [jnp.concatenate(parts_re, 1), jnp.concatenate(parts_im, 1)], 0
    )
    signal = dot(slow_inv[...], unturned)
    quarters, rows, _ = wide_ref.shape
    sources = rows // group
    for side in range(2):
        one = signal[:, side * LANES : (side + 1) * LANES]
        for q in range(quarters):
            wide_ref[q, pl.ds(chan + side, sources, stride=group), :] = one[
                q * sources : (q + 1) * sources
            ]


def collect(wide_ref, out_ref, first_row, group):
    for source in range(out_ref.shape[0]):
        out_ref[source, first_row : first_row + group, :] = jnp.concatenate(
            [
                wide_ref[quarter, source * group : (source + 1) * group, :]
                for quarter in range(wide_ref.shape[0])
            ],
            1,
        ).astype(BF16)


def conv_kernel(in_ref, *refs):
    tables = refs[:5]
    conv_ref, gated_ref, taps_ref, wide_gated, wide_taps, wide_out = refs[5:]
    group = conv_ref.shape[1]
    spread(in_ref, 0, wide_gated, group)
    spread(in_ref, group, wide_taps, group)
    for pair in range(group // 2):
        spec_gated = forward_pair(wide_gated, 2 * pair, group, tables)
        spec_taps = forward_pair(wide_taps, 2 * pair, group, tables)
        gated_ref[pair] = spec_gated
        taps_ref[pair] = spec_taps
        inverse_pair(product(spec_gated, spec_taps, False), 2 * pair, wide_out, group, tables)
    collect(wide_out, conv_ref, 0, group)


def grad_kernel(in_ref, gated_ref, taps_ref, *refs):
    tables = refs[:5]
    terms_ref, grad_ref, wide_dconv, wide_terms, wide_grad = refs[5:]
    group = grad_ref.shape[1]
    spread(in_ref, 2 * group, wide_dconv, group)
    for pair in range(group // 2):
        spec_dconv = forward_pair(wide_dconv, 2 * pair, group, tables)
        inverse_pair(
            product(gated_ref[pair], spec_dconv, True), 2 * pair, wide_terms, group, tables
        )
        inverse_pair(product(taps_ref[pair], spec_dconv, True), 2 * pair, wide_grad, group, tables)
    collect(wide_terms, terms_ref, 0, group)
    collect(wide_grad, grad_ref, 0, group)


def project_kernel(
    tensor_ref, conv_ref, query_ref, cot_ref, weight_ref, grad_ref, part_ref, gate_ref
):
    @pl.when(pl.program_id(0) == 0)
    def _():
        conv = flip(conv_ref[...].reshape(-1, conv_ref.shape[-1]))
        grad_ref[...] = times(cot_ref[...], conv)
        gate_ref[...] = times(query_ref[...], conv)

    part_ref[...] = dot(gate_ref[...], weight_ref[...]).astype(BF16)


def finish_kernel(scale, in_ref, key_ref, value_ref, value_grad_ref, key_grad_ref, taps_grad_ref):
    group = in_ref.shape[1] // 2
    grad = flip(in_ref[:, :group, :].reshape(-1, in_ref.shape[-1]))
    value_grad_ref[...] = times(grad, key_ref[...])
    key_grad_ref[...] = times(grad, value_ref[...])
    terms = flip(in_ref[:, group:, :].reshape(-1, in_ref.shape[-1]))
    taps_grad_ref[...] = terms.astype(F32) * scale


VMEM = pl.BlockSpec(memory_space=pltpu.VMEM)


def params():
    return pltpu.CompilerParams(vmem_limit_bytes=48 * 1024 * 1024)


def cost(flops, moved):
    return pl.CostEstimate(flops=flops, bytes_accessed=moved, transcendentals=0)


def shards(value_in, key_in, query_in, filter_taps, out_weight, cotangent):
    _, block, chans = value_in.shape
    sources = lax.axis_size("context")
    tensors = lax.axis_size("tensor")
    length = sources * block
    group = chans // sources
    radix = length // LANES
    value_in, key_in, query_in, cotangent = (
        one.reshape(block, chans) for one in (value_in, key_in, query_in, cotangent)
    )
    tables = right_angle_tables(sources, length)

    steps = chans // LANES
    slab = pl.BlockSpec((block, LANES), lambda step: (0, step))
    sent = pl.pallas_call(
        gate_kernel,
        grid=(steps,),
        in_specs=[slab] * 5,
        out_specs=pl.BlockSpec((sources // steps, 3 * group, block), lambda step: (step, 0, 0)),
        out_shape=jax.ShapeDtypeStruct((sources, 3 * group, block), BF16),
        compiler_params=params(),
        cost_estimate=cost(6 * block * chans * LANES, 8 * 2 * block * chans),
        name="gate_and_turn",
    )(value_in, key_in, query_in, cotangent, filter_taps)
    received = lax.all_to_all(sent, "context", 0, 0, tiled=True)

    piece = jax.ShapeDtypeStruct((sources, group, block), BF16)
    spectrum = jax.ShapeDtypeStruct((group // 2, 2 * radix, 2 * LANES), F32)
    wide = pltpu.VMEM((block // LANES, sources * group, LANES), F32)
    work = 6 * group * radix * LANES * 4 * LANES
    conv, spec_gated, spec_taps = pl.pallas_call(
        conv_kernel,
        in_specs=[VMEM] * 6,
        out_specs=[VMEM] * 3,
        out_shape=[piece, spectrum, spectrum],
        scratch_shapes=[wide] * 3,
        compiler_params=params(),
        cost_estimate=cost(work, 8 * 2**20),
        name="convolve",
    )(received, *tables)
    conv_back = lax.all_to_all(conv, "context", 0, 0, tiled=True)
    terms, grad = pl.pallas_call(
        grad_kernel,
        in_specs=[VMEM] * 8,
        out_specs=[VMEM] * 2,
        out_shape=[piece, piece],
        scratch_shapes=[wide] * 3,
        compiler_params=params(),
        cost_estimate=cost(work, 8 * 2**20),
        name="correlate",
    )(received, spec_gated, spec_taps, *tables)
    others = lax.ppermute(terms, "dp", [(0, 1), (1, 0)])

    where = lax.axis_index("tensor").astype(jnp.int32).reshape(1)
    grad_query, parts = pl.pallas_call(
        project_kernel,
        grid_spec=pltpu.PrefetchScalarGridSpec(
            num_scalar_prefetch=1,
            grid=(tensors,),
            in_specs=[
                pl.BlockSpec((sources, group, block), lambda step, at: (0, 0, 0)),
                pl.BlockSpec((block, chans), lambda step, at: (0, 0)),
                pl.BlockSpec((block, chans), lambda step, at: (0, 0)),
                pl.BlockSpec((chans, chans), lambda step, at: (0, (at[0] + step) % tensors)),
            ],
            out_specs=[
                pl.BlockSpec((block, chans), lambda step, at: (0, 0)),
                pl.BlockSpec((None, block, chans), lambda step, at: (step, 0, 0)),
            ],
            scratch_shapes=[pltpu.VMEM((block, chans), BF16)],
        ),
        out_shape=[
            jax.ShapeDtypeStruct((block, chans), BF16),
            jax.ShapeDtypeStruct((tensors, block, chans), BF16),
        ],
        compiler_params=params(),
        cost_estimate=cost(2 * block * chans * chans * tensors, 6 * 2**20),
        name="project",
    )(where, conv_back, query_in, cotangent, out_weight)
    total = parts[0].astype(F32)
    for offset in range(1, tensors):
        total = total + lax.ppermute(
            parts[offset], "tensor", [(one, (one + offset) % tensors) for one in range(tensors)]
        ).astype(F32)
    mixed_out = total.astype(BF16)

    terms_sum = (terms.astype(F32) + others.astype(F32)).astype(BF16)
    grads_back = lax.all_to_all(
        jnp.concatenate([grad, terms_sum], 1), "context", 0, 0, tiled=True
    )
    scale = 1.0 / math.sqrt(lax.axis_size("dp") * length)
    steps = block // LANES
    slab = pl.BlockSpec((LANES, chans), lambda step: (step, 0))
    grad_value, grad_key, grad_filter = pl.pallas_call(
        functools.partial(finish_kernel, scale),
        grid=(steps,),
        in_specs=[
            pl.BlockSpec((sources, 2 * group, LANES), lambda step: (0, 0, step)),
            slab,
            slab,
        ],
        out_specs=[slab] * 3,
        out_shape=[
            jax.ShapeDtypeStruct((block, chans), BF16),
            jax.ShapeDtypeStruct((block, chans), BF16),
            jax.ShapeDtypeStruct((block, chans), F32),
        ],
        compiler_params=params(),
        cost_estimate=cost(4 * block * chans * LANES, 10 * block * chans),
        name="finish",
    )(grads_back, key_in, value_in)
    return (
        mixed_out[None],
        grad_value[None],
        grad_key[None],
        grad_query[None],
        grad_filter,
    )


def solution(mesh):
    whole = P("dp", "context", "tensor")
    return jax.shard_map(
        shards,
        mesh=mesh,
        in_specs=(whole, whole, whole, P("context", "tensor"), P("tensor", None), whole),
        out_specs=(whole, whole, whole, whole, P("context", "tensor")),
        check_vma=False,
    )
```

time: 390 us -> 155 us (0.40)
  the two profiles are of different devices: /device:TPU:1 before, /device:TPU:163 now
where the time goes in v1:
time: 155 us; the launch traced here: 154 us
  waiting for transfers between devices  66.1 us (43%)
  blocking collectives  29.8 us (19%)
  Pallas kernels  21.7 us (14%)
  local copies, waits for them, and re-layouts  16.6 us (11%)
  starting transfers between devices  15.4 us (10%)
  other arithmetic  3.35 us (2%)
    ppermute x3, waiting for transfers between devices, shards(): lax.ppermute(parts[offset], 'tensor', [(one, (one + offset) % tensors) fo...  46.1 us
    all_to_all x1, blocking collectives, shards(): received = lax.all_to_all(sent, 'context', 0, 0, tiled=True)  29.8 us
    ppermute x1, waiting for transfers between devices, shards(): others = lax.ppermute(terms, 'dp', [(0, 1), (1, 0)])  20 us
    unnamed x42, local copies, waits for them, and re-layouts  16.5 us
    pallas_call x1, Pallas kernels, shards(): pl.pallas_call(grad_kernel, in_specs=[VMEM] * 8, out_specs=[VMEM] * 2, ou...  8.46 us
    all_to_all x1, starting transfers between devices, shards(): lax.all_to_all(jnp.concatenate([grad, terms_sum], 1), 'context', 0, 0, ti...  8.31 us
    pallas_call x1, Pallas kernels, shards(): pl.pallas_call(conv_kernel, in_specs=[VMEM] * 6, out_specs=[VMEM] * 3, ou...  6.16 us
    all_to_all x1, starting transfers between devices, shards(): conv_back = lax.all_to_all(conv, 'context', 0, 0, tiled=True)  4.84 us
  transfers between devices with their start and end apart: 6, of which 4 were waited for; matrix products, arithmetic and copies ran while one was open for 1% of the time, Pallas kernels for 7%

profile of v1, /device:TPU:163, one launch (start us, length us, event | category | flops | bytes accessed | tf_op | source)
XLA Modules:
  0.0 153.8 jit_solution(1555428588120899454)
XLA Ops:
  0.6 0.0 copy-start.2
  0.6 1.0 copy-done.2
  1.7 1.0 copy-done.4
  2.7 1.0 copy-done.10
  3.8 1.0 copy-done.11
  4.8 1.0 copy-done.13
  5.8 1.7 %gate_and_turn.1 = bf16[32,48,512]{2,1,0:T(8,128)(2,1)S(1)} custom-call(bf16[512,512]{1,0:T(8,128)(2,1)S(1)} %bitcast.19, bf16[512,512]{1,0:T(8,128)(2,1)S(1)} %bitcast.21, bf16[512,512]{1,0:T(8,128)(2,1)S(1)} %bitcast.23, bf16[512,512]{1,0:T(8,128)(2,1)S(1)} %bitcast.25, bf16[512,512]{1,0:T(8,128)(2,1)S(1)} %copy-done.10), custom_call_target="tpu_custom_call" | custom-call | flops 201326592 | bytes 4194304 | tf_op jit(solution)/shard_map/gate_and_turn/pallas_call | solution.py:235
  7.5 0.0 copy-start.15
  7.5 0.0 copy-start.16
  7.5 0.0 copy-start.17
  7.5 0.0 copy-start.18
  7.6 0.0 copy-start.19
  7.6 29.8 %all_to_all.15.in_ref = bf16[32,48,512]{2,1,0:T(8,128)(2,1)S(1)} all-to-all(bf16[32,48,512]{2,1,0:T(8,128)(2,1)S(1)} %gate_and_turn.1), channel_id=1, replica_groups=mesh['dp'=2,'context'=32,'tensor'=4] {'context'}, dimensions={0} | all-to-all | bytes 3145728 | tf_op jit(solution)/shard_map/all_to_all | solution.py:245
  37.4 0.0 copy-done.15
  37.4 0.0 copy-done.16
  37.4 0.0 copy-done.17
  37.4 0.0 copy-done.18
  37.4 0.0 copy-done.19
  37.4 6.2 %convolve.1 = (bf16[32,16,512]{2,1,0:T(8,128)(2,1)}, f32[8,256,256]{2,1,0:T(8,128)S(1)}, f32[8,256,256]{2,1,0:T(8,128)}) custom-call(bf16[32,48,512]{2,1,0:T(8,128)(2,1)S(1)} %all_to_all.15.in_ref, bf16[256,128]{1,0:T(8,128)(2,1)S(1)} %copy-done.18, bf16[256,256]{1,0:T(8,128)(2,1)S(1)} %copy-done.16, bf16[256,256]{1,0:T(8,128)(2,1)S(1)} %copy-done.17, ...), custom_call_target="tpu_custom_call" | custom-call | flops 805306368 | bytes 8388608 | tf_op jit(solution)/shard_map/convolve/pallas_call | solution.py:251
  43.6 1.3 copy-done
  44.9 4.8 %all-to-all-start.1 = ((bf16[32,16,512]{2,1,0:T(8,128)(2,1)}), bf16[32,16,512]{2,1,0:T(8,128)(2,1)S(1)}, u32[]{:S(2)}, u32[]{:S(2)}) async-start(bf16[32,16,512]{2,1,0:T(8,128)(2,1)} %get-tuple-element.15), calls=%async_computation.1 | async-start | bytes 1048576 | tf_op jit(solution)/shard_map/all_to_all | solution.py:261
  49.8 1.6 %copy-done.1 = f32[8,256,256]{2,1,0:T(8,128)S(1)} copy-done((f32[8,256,256]{2,1,0:T(8,128)S(1)}, f32[8,256,256]{2,1,0:T(8,128)}, u32[]{:S(2)}) %copy-start.1) | copy-done | bytes 2097176
  51.3 8.5 %correlate.1 = (bf16[32,16,512]{2,1,0:T(8,128)(2,1)}, bf16[32,16,512]{2,1,0:T(8,128)(2,1)S(1)}) custom-call(bf16[32,48,512]{2,1,0:T(8,128)(2,1)S(1)} %all_to_all.15.in_ref, f32[8,256,256]{2,1,0:T(8,128)S(1)} %copy-done.1, f32[8,256,256]{2,1,0:T(8,128)} %get-tuple-element.18.taps_ref, bf16[256,128]{1,0:T(8,128)(2,1)S(1)} %copy-done.18, ...), custom_call_target="tpu_custom_call" | custom-call | flops 805306368 | bytes 8388608 | tf_op jit(solution)/shard_map/correlate/pallas_call | solution.py:262
  59.8 0.8 copy-done.8
  60.6 0.0 collective-permute-start.3
  60.6 0.0 all-to-all-done.1.conv_ref
  60.6 0.8 copy-done.6
  61.4 1.0 copy-done.7
  62.4 1.0 copy-done.12
  63.5 1.0 copy-done.14
  64.5 1.6 %copy-done.20 = bf16[512,2048]{1,0:T(8,128)(2,1)S(1)} copy-done((bf16[512,2048]{1,0:T(8,128)(2,1)S(1)}, bf16[512,2048]{1,0:T(8,128)(2,1)}, u32[]{:S(2)}) %copy-start.20) | copy-done | bytes 2097176
  66.1 3.0 %project.1 = (bf16[512,512]{1,0:T(8,128)(2,1)}, bf16[4,512,512]{2,1,0:T(8,128)(2,1)S(1)}) custom-call(s32[1]{0:T(128)} %bitcast.tensor_ref, bf16[32,16,512]{2,1,0:T(8,128)(2,1)S(1)} %copy-done.7, bf16[512,512]{1,0:T(8,128)(2,1)S(1)} %bitcast.24, bf16[512,512]{1,0:T(8,128)(2,1)S(1)} %bitcast.26, bf16[512,2048]{1,0:T(8,128)(2,1)S(1)} %copy-done.20), custom_call_target="tpu_custom_call" | custom-call | flops 1073741824 | bytes 6291456 | tf_op jit(solution)/shard_map/project/pallas_call | solution.py:275
  69.1 20.0 %collective-permute-done.3 = bf16[32,16,512]{2,1,0:T(8,128)(2,1)S(1)} collective-permute-done((bf16[32,16,512]{2,1,0:T(8,128)(2,1)}, bf16[32,16,512]{2,1,0:T(8,128)(2,1)S(1)}, u32[]{:S(2)}, u32[]{:S(2)}) %collective-permute-start.3) | collective-permute-done | bytes 524320 | tf_op jit(solution)/shard_map/ppermute | solution.py:272
  89.1 1.2 add_convert_fusion
  90.3 1.1 pad_maximum_fusion
  91.4 8.3 %all-to-all-start.2 = ((bf16[32,32,512]{2,1,0:T(8,128)(2,1)}), bf16[32,32,512]{2,1,0:T(8,128)(2,1)S(1)}, u32[]{:S(2)}, u32[]{:S(2)}) async-start(bf16[32,32,512]{2,1,0:T(8,128)(2,1)} %pad_maximum_fusion), calls=%async_computation.2 | async-start | bytes 2097152 | tf_op jit(solution)/shard_map/all_to_all | solution.py:308
  99.7 0.1 slice_bitcast_fusion.2
  99.8 0.6 collective-permute-start
  100.5 1.6 %collective-permute-start.1 = (bf16[512,512]{1,0:T(8,128)(2,1)S(1)}, bf16[512,512]{1,0:T(8,128)(2,1)S(1)}, u32[]{:S(2)}, u32[]{:S(2)}) collective-permute-start(bf16[512,512]{1,0:T(8,128)(2,1)S(1)} %get-tuple-element.27), channel_id=1, source_target_pairs={{0,2},{1,3},{2,0},{3,1},{4,6},{5,7},{6,4},{7,5},{8,10},{9,11},{10,... | collective-permute-start | bytes 1572872 | tf_op jit(solution)/shard_map/ppermute | solution.py:302
  102.1 0.0 collective-permute-start.2
  102.1 10.9 %collective-permute-done = bf16[512,512]{1,0:T(8,128)(2,1)S(1)} collective-permute-done((bf16[512,512]{1,0:T(8,128)(2,1)S(1)}, bf16[512,512]{1,0:T(8,128)(2,1)S(1)}, u32[]{:S(2)}, u32[]{:S(2)}) %collective-permute-start) | collective-permute-done | bytes 524320 | tf_op jit(solution)/shard_map/ppermute | solution.py:302
  113.1 32.1 %collective-permute-done.1 = bf16[512,512]{1,0:T(8,128)(2,1)S(1)} collective-permute-done((bf16[512,512]{1,0:T(8,128)(2,1)S(1)}, bf16[512,512]{1,0:T(8,128)(2,1)S(1)}, u32[]{:S(2)}, u32[]{:S(2)}) %collective-permute-start.1) | collective-permute-done | bytes 524320 | tf_op jit(solution)/shard_map/ppermute | solution.py:302
  145.1 3.1 %collective-permute-done.2 = bf16[512,512]{1,0:T(8,128)(2,1)S(1)} collective-permute-done((bf16[512,512]{1,0:T(8,128)(2,1)S(1)}, bf16[512,512]{1,0:T(8,128)(2,1)S(1)}, u32[]{:S(2)}, u32[]{:S(2)}) %collective-permute-start.2) | collective-permute-done | bytes 524320 | tf_op jit(solution)/shard_map/ppermute | solution.py:302
  148.2 1.1 fusion.3
  149.3 0.0 all-to-all-done.2.in_ref
  149.3 1.0 copy-done.3
  150.3 1.0 copy-done.5
  151.4 2.4 %finish.1 = (bf16[512,512]{1,0:T(8,128)(2,1)}, bf16[512,512]{1,0:T(8,128)(2,1)}, f32[512,512]{1,0:T(8,128)}) custom-call(bf16[32,32,512]{2,1,0:T(8,128)(2,1)S(1)} %all-to-all-done.2.in_ref, bf16[512,512]{1,0:T(8,128)(2,1)S(1)} %bitcast.22, bf16[512,512]{1,0:T(8,128)(2,1)S(1)} %bitcast.20), custom_call_target="tpu_custom_call" | custom-call | flops 134217728 | bytes 2621440 | tf_op jit(solution)/shard_map/finish/pallas_call | solution.py:314
  (16 shorter events, 0.0 us)
Async XLA Ops:
  0.6 1.0 copy-start.2
  1.7 1.0 copy-start.4
  2.7 1.0 copy-start.10
  3.8 1.0 copy-start.11
  4.8 1.0 copy-start.13
  7.5 29.9 %copy-start.15 = (f32[4,128,128]{2,1,0:T(8,128)S(1)}, f32[4,128,128]{2,1,0:T(8,128)}, u32[]{:S(2)}) copy-start(f32[4,128,128]{2,1,0:T(8,128)} %constant.18.clone.refs_4_) | copy-start | bytes 786436
  7.5 29.9 %copy-start.16 = (bf16[256,256]{1,0:T(8,128)(2,1)S(1)}, bf16[256,256]{1,0:T(8,128)(2,1)}, u32[]{:S(2)}) copy-start(bf16[256,256]{1,0:T(8,128)(2,1)} %constant.15.clone.refs_1_) | copy-start | bytes 393220
  7.5 29.9 %copy-start.17 = (bf16[256,256]{1,0:T(8,128)(2,1)S(1)}, bf16[256,256]{1,0:T(8,128)(2,1)}, u32[]{:S(2)}) copy-start(bf16[256,256]{1,0:T(8,128)(2,1)} %constant.16.clone.refs_2_) | copy-start | bytes 393220
  7.5 29.9 %copy-start.18 = (bf16[256,128]{1,0:T(8,128)(2,1)S(1)}, bf16[256,128]{1,0:T(8,128)(2,1)}, u32[]{:S(2)}) copy-start(bf16[256,128]{1,0:T(8,128)(2,1)} %constant.14.clone.refs_0_) | copy-start | bytes 196612
  7.6 29.9 %copy-start.19 = (bf16[128,256]{1,0:T(8,128)(2,1)S(1)}, bf16[128,256]{1,0:T(8,128)(2,1)}, u32[]{:S(2)}) copy-start(bf16[128,256]{1,0:T(8,128)(2,1)} %constant.17.clone.refs_3_) | copy-start | bytes 196612
  43.6 1.3 copy-start
  44.9 15.7 %all-to-all-start.1 = ((bf16[32,16,512]{2,1,0:T(8,128)(2,1)}), bf16[32,16,512]{2,1,0:T(8,128)(2,1)S(1)}, u32[]{:S(2)}, u32[]{:S(2)}) async-start(bf16[32,16,512]{2,1,0:T(8,128)(2,1)} %get-tuple-element.15), calls=%async_computation.1 | async-start | bytes 1048576 | tf_op jit(solution)/shard_map/all_to_all | solution.py:261
  49.7 1.6 %copy-start.1 = (f32[8,256,256]{2,1,0:T(8,128)S(1)}, f32[8,256,256]{2,1,0:T(8,128)}, u32[]{:S(2)}) copy-start(f32[8,256,256]{2,1,0:T(8,128)} %copy-done) | copy-start | bytes 6291460
  59.8 0.8 copy-start.8
  60.6 28.5 %collective-permute-start.3 = (bf16[32,16,512]{2,1,0:T(8,128)(2,1)}, bf16[32,16,512]{2,1,0:T(8,128)(2,1)S(1)}, u32[]{:S(2)}, u32[]{:S(2)}) collective-permute-start(bf16[32,16,512]{2,1,0:T(8,128)(2,1)} %get-tuple-element.20), channel_id=1, source_target_pairs={{0,128},{128,0},{1,129},{129,1},{2,130},{130,2},{3,131},{131,3},{4... | collective-permute-start | bytes 1572872 | tf_op jit(solution)/shard_map/ppermute | solution.py:272
  60.6 0.8 copy-start.6
  61.4 1.0 copy-start.7
  62.4 1.0 copy-start.12
  63.5 1.0 copy-start.14
  64.5 1.6 %copy-start.20 = (bf16[512,2048]{1,0:T(8,128)(2,1)S(1)}, bf16[512,2048]{1,0:T(8,128)(2,1)}, u32[]{:S(2)}) copy-start(bf16[512,2048]{1,0:T(8,128)(2,1)} %weight_ref.1) | copy-start | bytes 6291460
  66.1 24.2 %copy-start.9 = (bf16[32,16,512]{2,1,0:T(8,128)(2,1)S(1)}, bf16[32,16,512]{2,1,0:T(8,128)(2,1)}, u32[]{:S(2)}) copy-start(bf16[32,16,512]{2,1,0:T(8,128)(2,1)} %copy-done.8) | copy-start | bytes 1572868
  91.4 57.9 %all-to-all-start.2 = ((bf16[32,32,512]{2,1,0:T(8,128)(2,1)}), bf16[32,32,512]{2,1,0:T(8,128)(2,1)S(1)}, u32[]{:S(2)}, u32[]{:S(2)}) async-start(bf16[32,32,512]{2,1,0:T(8,128)(2,1)} %pad_maximum_fusion), calls=%async_computation.2 | async-start | bytes 2097152 | tf_op jit(solution)/shard_map/all_to_all | solution.py:308
  99.8 13.2 %collective-permute-start = (bf16[512,512]{1,0:T(8,128)(2,1)S(1)}, bf16[512,512]{1,0:T(8,128)(2,1)S(1)}, u32[]{:S(2)}, u32[]{:S(2)}) collective-permute-start(bf16[512,512]{1,0:T(8,128)(2,1)S(1)} %get-tuple-element.25), channel_id=1, source_target_pairs={{0,1},{1,2},{2,3},{3,0},{4,5},{5,6},{6,7},{7,4},{8,9},{9,10},{10,1... | collective-permute-start | bytes 1572872 | tf_op jit(solution)/shard_map/ppermute | solution.py:302
  100.5 44.7 %collective-permute-start.1 = (bf16[512,512]{1,0:T(8,128)(2,1)S(1)}, bf16[512,512]{1,0:T(8,128)(2,1)S(1)}, u32[]{:S(2)}, u32[]{:S(2)}) collective-permute-start(bf16[512,512]{1,0:T(8,128)(2,1)S(1)} %get-tuple-element.27), channel_id=1, source_target_pairs={{0,2},{1,3},{2,0},{3,1},{4,6},{5,7},{6,4},{7,5},{8,10},{9,11},{10,... | collective-permute-start | bytes 1572872 | tf_op jit(solution)/shard_map/ppermute | solution.py:302
  102.1 46.1 %collective-permute-start.2 = (bf16[512,512]{1,0:T(8,128)(2,1)S(1)}, bf16[512,512]{1,0:T(8,128)(2,1)S(1)}, u32[]{:S(2)}, u32[]{:S(2)}) collective-permute-start(bf16[512,512]{1,0:T(8,128)(2,1)S(1)} %get-tuple-element.26), channel_id=1, source_target_pairs={{0,3},{1,0},{2,1},{3,2},{4,7},{5,4},{6,5},{7,6},{8,11},{9,8},{10,9... | collective-permute-start | bytes 1572872 | tf_op jit(solution)/shard_map/ppermute | solution.py:302
  149.3 1.0 copy-start.3
  150.3 1.0 copy-start.5

commit v2 on v1

v2 whole, which is shorter than its diff:
```python
import functools
import math

import jax
import jax.numpy as jnp
import numpy as np
from jax import lax
from jax.experimental import pallas as pl
from jax.experimental.pallas import tpu as pltpu
from jax.sharding import PartitionSpec as P

LANES = 128
F32 = jnp.float32
BF16 = jnp.bfloat16
SMALL = 16
MIDDLE = 36
ADD = 60
PROJECT = 60


def right_angle_tables(source_count, length):
    radix = length // LANES
    quarters = radix // source_count
    row = np.arange(radix)
    slow = (row % source_count) * quarters + row // source_count
    freq = np.arange(radix) + 0.25
    slow_angle = -2.0 * np.pi * freq[:, None] * slow[None, :] / radix
    slow_fwd = np.concatenate([np.cos(slow_angle), np.sin(slow_angle)], 0)
    slow_inv = slow_fwd.T
    fast = np.arange(LANES)
    turn_angle = -2.0 * np.pi * freq[:, None] * fast[None, :] / length
    turn_cos, turn_sin = np.cos(turn_angle), np.sin(turn_angle)
    fast_angle = -2.0 * np.pi * ((fast[:, None] * fast[None, :]) % LANES) / LANES
    fast_cos, fast_sin = np.cos(fast_angle), np.sin(fast_angle)
    fast_fwd = np.block([[fast_cos, fast_sin], [-fast_sin, fast_cos]])
    fast_inv = np.block([[fast_cos, -fast_sin], [fast_sin, fast_cos]])
    turn = np.stack([turn_cos, turn_sin, turn_cos / length, turn_sin / length])
    slow_fwd = np.concatenate([slow_fwd, np.zeros_like(slow_fwd)], 1)
    factors = np.concatenate([slow_fwd, fast_fwd, fast_inv, slow_inv], 0)
    return (jnp.asarray(factors, BF16), jnp.asarray(turn, F32))


def factors_of(factors_ref):
    size = 2 * LANES
    return (
        factors_ref.at[:size, :LANES],
        factors_ref.at[size : 2 * size, :],
        factors_ref.at[2 * size : 3 * size, :],
        factors_ref.at[3 * size :, :],
    )


def dot(left, right):
    return jnp.dot(left, right, preferred_element_type=F32)


def flip(square):
    extent = square.shape[1]
    rows = lax.broadcasted_iota(jnp.int32, (extent, extent), 0)
    cols = lax.broadcasted_iota(jnp.int32, (extent, extent), 1)
    unit = jnp.where(rows == cols, 1.0, 0.0).astype(BF16)
    turned = lax.dot_general(unit, square, (((1,), (1,)), ((), ())), preferred_element_type=F32)
    return turned.astype(BF16)


def times(left, right):
    return (left.astype(F32) * right.astype(F32)).astype(BF16)


def gate_kernel(*refs):
    in_refs, (out_ref, held, arrival) = refs[:5], refs[5:]
    _, chunks, _, width = held.shape

    def copy(one, chunk):
        return pltpu.make_async_copy(
            in_refs[one].at[:, pl.ds(chunk * width, width)],
            held.at[one, chunk],
            arrival.at[one, chunk],
        )

    for chunk in range(chunks):
        for one in range(5):
            copy(one, chunk).start()
    group = out_ref.shape[1] // 3
    share = out_ref.shape[0] // chunks
    for chunk in range(chunks):
        for one in range(5):
            copy(one, chunk).wait()
        value, key, query, cotangent, taps = (held[one, chunk] for one in range(5))
        for slot, signal in enumerate((times(key, value), taps, times(cotangent, query))):
            turned = flip(signal)
            out_ref[
                chunk * share : (chunk + 1) * share, slot * group : (slot + 1) * group, :
            ] = turned.reshape(share, group, turned.shape[1])


def spread(in_ref, first_row, wide_ref, group):
    for source in range(in_ref.shape[0]):
        rows = in_ref[source, first_row : first_row + group, :].astype(F32)
        for quarter in range(wide_ref.shape[0]):
            wide_ref[quarter, source * group : (source + 1) * group, :] = rows[
                :, quarter * LANES : (quarter + 1) * LANES
            ]


def turn_forward(wide_ref, turned_ref, group, slow_fwd, turn):
    quarters, rows, _ = wide_ref.shape
    turn_cos, turn_sin = turn[0], turn[1]
    for chan in range(0, group, 2):
        columns = [
            jnp.concatenate(
                [wide_ref[q, pl.ds(one, rows // group, stride=group), :] for q in range(quarters)],
                0,
            )
            for one in (chan, chan + 1)
        ]
        first = dot(slow_fwd[...], jnp.concatenate(columns, 1).astype(BF16))
        radix = first.shape[0] // 2
        for side in range(2):
            lanes = slice(side * LANES, (side + 1) * LANES)
            part_re, part_im = first[:radix, lanes], first[radix:, lanes]
            out_rows = slice((chan + side) * radix, (chan + side + 1) * radix)
            turned_ref[out_rows, :LANES] = (part_re * turn_cos - part_im * turn_sin).astype(BF16)
            turned_ref[out_rows, LANES:] = (part_re * turn_sin + part_im * turn_cos).astype(BF16)


def product(left, right, conjugate):
    left_re, left_im = left[:, :LANES], left[:, LANES:]
    right_re, right_im = right[:, :LANES], right[:, LANES:]
    if conjugate:
        both_re = left_re * right_re + left_im * right_im
        both_im = left_re * right_im - left_im * right_re
    else:
        both_re = left_re * right_re - left_im * right_im
        both_im = left_re * right_im + left_im * right_re
    return jnp.concatenate([both_re, both_im], 1).astype(BF16)


def invert(spectrum_ref, back_ref, wide_ref, group, fast_inv, slow_inv, turn):
    back_ref[...] = dot(spectrum_ref[...], fast_inv[...])
    quarters, rows, _ = wide_ref.shape
    sources = rows // group
    radix = back_ref.shape[0] // group
    turn_cos, turn_sin = turn[2], turn[3]
    for chan in range(0, group, 2):
        parts_re, parts_im = [], []
        for one in (chan, chan + 1):
            in_rows = slice(one * radix, (one + 1) * radix)
            back_re, back_im = back_ref[in_rows, :LANES], back_ref[in_rows, LANES:]
            parts_re.append((back_re * turn_cos + back_im * turn_sin).astype(BF16))
            parts_im.append((back_im * turn_cos - back_re * turn_sin).astype(BF16))
        unturned = jnp.concatenate(
            [jnp.concatenate(parts_re, 1), jnp.concatenate(parts_im, 1)], 0
        )
        signal = dot(slow_inv[...], unturned)
        for side in range(2):
            one = signal[:, side * LANES : (side + 1) * LANES]
            for q in range(quarters):
                wide_ref[q, pl.ds(chan + side, sources, stride=group), :] = one[
                    q * sources : (q + 1) * sources
                ]


def collect(wide_ref, out_ref, group):
    for source in range(out_ref.shape[0]):
        out_ref[source, :group, :] = jnp.concatenate(
            [
                wide_ref[quarter, source * group : (source + 1) * group, :]
                for quarter in range(wide_ref.shape[0])
            ],
            1,
        ).astype(BF16)


def transform_kernel(in_ref, factors_ref, turn, *refs):
    slow_fwd, fast_fwd, fast_inv, slow_inv = factors_of(factors_ref)
    out_refs, (wide, turned, spectra, mixed, back) = refs[:3], refs[3:]
    group = out_refs[0].shape[1]
    for slot in range(3):
        spread(in_ref, slot * group, wide.at[slot], group)
        turn_forward(wide.at[slot], turned.at[slot], group, slow_fwd, turn)
        spectra[slot] = dot(turned[slot], fast_fwd[...])
    rows = spectra.shape[1] // group
    for chan in range(group):
        part = slice(chan * rows, (chan + 1) * rows)
        gated, taps, dconv = (spectra[slot, part, :] for slot in range(3))
        mixed[0, part, :] = product(gated, taps, False)
        mixed[1, part, :] = product(gated, dconv, True)
        mixed[2, part, :] = product(taps, dconv, True)
    for slot, out_ref in enumerate(out_refs):
        invert(mixed.at[slot], back.at[slot], wide.at[slot], group, fast_inv, slow_inv, turn)
        collect(wide.at[slot], out_ref, group)


def add_kernel(*refs):
    total = refs[0][...].astype(F32)
    for one in refs[1:-1]:
        total = total + one[...].astype(F32)
    refs[-1][...] = total.astype(BF16)


def join_kernel(upper_ref, lower_ref, out_ref):
    group = upper_ref.shape[1]
    out_ref[:, :group, :] = upper_ref[...]
    out_ref[:, group:, :] = lower_ref[...]


def project_kernel(order_ref, conv_ref, query_ref, cot_ref, weight_ref, *out_refs):
    chans = query_ref.shape[1]
    gates = []
    for step in range(query_ref.shape[0] // LANES):
        rows = slice(step * LANES, (step + 1) * LANES)
        conv = flip(conv_ref[:, :, rows].reshape(-1, LANES))
        out_refs[4][rows, :] = times(cot_ref[rows, :], conv)
        gates.append(times(query_ref[rows, :], conv))
    for slot in range(4):
        columns = pl.ds(pl.multiple_of(order_ref[slot] * chans, chans), chans)
        for step, gate_out in enumerate(gates):
            rows = slice(step * LANES, (step + 1) * LANES)
            out_refs[slot][rows, :] = dot(gate_out, weight_ref[:, columns]).astype(BF16)


def finish_kernel(scale, in_ref, key_ref, value_ref, value_grad_ref, key_grad_ref, taps_grad_ref):
    group = in_ref.shape[1] // 2
    grad = flip(in_ref[:, :group, :].reshape(-1, in_ref.shape[-1]))
    value_grad_ref[...] = times(grad, key_ref[...])
    key_grad_ref[...] = times(grad, value_ref[...])
    terms = flip(in_ref[:, group:, :].reshape(-1, in_ref.shape[-1]))
    taps_grad_ref[...] = terms.astype(F32) * scale


VMEM = pl.BlockSpec(memory_space=pltpu.VMEM)
HBM = pl.BlockSpec(memory_space=pltpu.HBM)


def params(mebibytes=60):
    return pltpu.CompilerParams(vmem_limit_bytes=mebibytes * 1024 * 1024)


def cost(flops, moved):
    return pl.CostEstimate(flops=flops, bytes_accessed=moved, transcendentals=0)


def add_arrays(arrays, flops, name):
    return pl.pallas_call(
        add_kernel,
        in_specs=[VMEM] * len(arrays),
        out_specs=VMEM,
        out_shape=jax.ShapeDtypeStruct(arrays[0].shape, BF16),
        compiler_params=params(SMALL),
        cost_estimate=cost(flops, 2 * arrays[0].size * (len(arrays) + 1)),
        name=name,
    )(*arrays)


def shards(value_in, key_in, query_in, filter_taps, out_weight, cotangent):
    _, block, chans = value_in.shape
    sources = lax.axis_size("context")
    tensors = lax.axis_size("tensor")
    length = sources * block
    group = chans // sources
    radix = length // LANES
    value_in, key_in, query_in, cotangent = (
        one.reshape(block, chans) for one in (value_in, key_in, query_in, cotangent)
    )
    tables = right_angle_tables(sources, length)

    steps = chans // LANES
    sent = pl.pallas_call(
        gate_kernel,
        in_specs=[HBM] * 5,
        out_specs=VMEM,
        out_shape=jax.ShapeDtypeStruct((sources, 3 * group, block), BF16),
        scratch_shapes=[
            pltpu.VMEM((5, steps, block, LANES), BF16),
            pltpu.SemaphoreType.DMA((5, steps)),
        ],
        compiler_params=params(),
        cost_estimate=cost(6 * block * chans * LANES, 8 * 2 * block * chans),
        name="gate_and_turn",
    )(value_in, key_in, query_in, cotangent, filter_taps)
    received = lax.all_to_all(sent, "context", 0, 0, tiled=True)

    piece = jax.ShapeDtypeStruct((sources, group, block), BF16)
    rows = group * radix
    spectrum = (rows, 2 * LANES)
    wide = (block // LANES, sources * group, LANES)
    work = 6 * group * radix * LANES * 4 * LANES
    conv, terms, grad = pl.pallas_call(
        transform_kernel,
        in_specs=[VMEM] * 3,
        out_specs=[VMEM] * 3,
        out_shape=[piece] * 3,
        scratch_shapes=[
            pltpu.VMEM((3,) + wide, F32),
            pltpu.VMEM((3,) + spectrum, BF16),
            pltpu.VMEM((3,) + spectrum, F32),
            pltpu.VMEM((3,) + spectrum, BF16),
            pltpu.VMEM((3,) + spectrum, F32),
        ],
        compiler_params=params(MIDDLE),
        cost_estimate=cost(work, 8 * 2**20),
        name="transform",
    )(received, *tables)
    conv_back = lax.all_to_all(conv, "context", 0, 0, tiled=True)
    others = lax.ppermute(terms, "dp", [(0, 1), (1, 0)])

    at = lax.axis_index("tensor").astype(jnp.int32)
    last = tensors - 1
    mirrored = at > last - at

    def toward(chunk):
        return jnp.where(mirrored, last - chunk, chunk)

    outer = (at == 0) | (at == last)
    order = jnp.stack(
        [
            toward(3),
            jnp.where(outer, toward(1), toward(2)),
            jnp.where(outer, toward(2), toward(0)),
            at,
        ]
    )
    steps = block // LANES
    square = jax.ShapeDtypeStruct((block, chans), BF16)
    slab = pl.BlockSpec((LANES, chans), lambda step: (step, 0))
    far, near, other, own, grad_query = pl.pallas_call(
        project_kernel,
        in_specs=[pl.BlockSpec(memory_space=pltpu.SMEM)] + [VMEM] * 4,
        out_specs=[VMEM] * 5,
        out_shape=[square] * 5,
        compiler_params=params(SMALL),
        cost_estimate=cost(2 * block * chans * chans * tensors, 6 * 2**20),
        name="project",
    )(order, conv_back, query_in, cotangent, out_weight)
    relayed = lax.ppermute(far, "tensor", [(0, 1), (3, 2)])
    across = lax.ppermute(near, "tensor", [(1, 2), (2, 1)])
    beside = lax.ppermute(other, "tensor", [(0, 2), (3, 1), (1, 0), (2, 3)])
    inward = lax.ppermute(near, "tensor", [(0, 1), (3, 2)])
    terms_sum = add_arrays((terms, others), 2 * 10**9, "sum_terms")
    terms_sum, relayed = lax.optimization_barrier((terms_sum, relayed))
    both = add_arrays((far, relayed), 10**11, "relay")
    terms_sum, both = lax.optimization_barrier((terms_sum, both))
    outward = lax.ppermute(both, "tensor", [(1, 3), (2, 0)])
    joined = pl.pallas_call(
        join_kernel,
        in_specs=[VMEM] * 2,
        out_specs=VMEM,
        out_shape=jax.ShapeDtypeStruct((sources, 2 * group, block), BF16),
        compiler_params=params(SMALL),
        cost_estimate=cost(10**11, 4 * 2 * block * chans),
        name="join",
    )(grad, terms_sum)
    mixed_out = add_arrays(
        (own, across, beside, inward, outward), 10**11, "add_parts"
    )
    grads_back = lax.all_to_all(joined, "context", 0, 0, tiled=True)
    scale = 1.0 / math.sqrt(lax.axis_size("dp") * length)
    grad_value, grad_key, grad_filter = pl.pallas_call(
        functools.partial(finish_kernel, scale),
        grid=(steps,),
        in_specs=[
            pl.BlockSpec((sources, 2 * group, LANES), lambda step: (0, 0, step)),
            slab,
            slab,
        ],
        out_specs=[slab] * 3,
        out_shape=[
            jax.ShapeDtypeStruct((block, chans), BF16),
            jax.ShapeDtypeStruct((block, chans), BF16),
            jax.ShapeDtypeStruct((block, chans), F32),
        ],
        compiler_params=params(SMALL),
        cost_estimate=cost(4 * block * chans * LANES, 10 * block * chans),
        name="finish",
    )(grads_back, key_in, value_in)
    return (
        mixed_out[None],
        grad_value[None],
        grad_key[None],
        grad_query[None],
        grad_filter,
    )


def solution(mesh):
    whole = P("dp", "context", "tensor")
    return jax.shard_map(
        shards,
        mesh=mesh,
        in_specs=(whole, whole, whole, P("context", "tensor"), P("tensor", None), whole),
        out_specs=(whole, whole, whole, whole, P("context", "tensor")),
        check_vma=False,
    )
```

time: 155 us -> 119 us (0.77)
  the two profiles are of different devices: /device:TPU:163 before, /device:TPU:1 now
where the time goes in v2:
time: 119 us; the launch traced here: 118 us
  waiting for transfers between devices  33.6 us (28%)
  blocking collectives  31.5 us (26%)
  starting transfers between devices  30.5 us (26%)
  Pallas kernels  19 us (16%)
  local copies, waits for them, and re-layouts  2.42 us (2%)
    all_to_all x1, blocking collectives, shards(): received = lax.all_to_all(sent, 'context', 0, 0, tiled=True)  31.5 us
    ppermute x1, waiting for transfers between devices, shards(): relayed = lax.ppermute(far, 'tensor', [(0, 1), (3, 2)])  14.4 us
    ppermute x1, waiting for transfers between devices, shards(): beside = lax.ppermute(other, 'tensor', [(0, 2), (3, 1), (1, 0), (2, 3)])  11 us
    all_to_all x1, starting transfers between devices, shards(): grads_back = lax.all_to_all(joined, 'context', 0, 0, tiled=True)  9.12 us
    ppermute x1, starting transfers between devices, shards(): others = lax.ppermute(terms, 'dp', [(0, 1), (1, 0)])  7 us
    pallas_call x1, Pallas kernels, shards(): pl.pallas_call(transform_kernel, in_specs=[VMEM] * 3, out_specs=[VMEM] *...  6.19 us
    all_to_all x1, waiting for transfers between devices, shards(): conv_back = lax.all_to_all(conv, 'context', 0, 0, tiled=True)  4.58 us
    ppermute x1, starting transfers between devices, shards(): inward = lax.ppermute(near, 'tensor', [(0, 1), (3, 2)])  4.1 us
  transfers between devices with their start and end apart: 8, of which 5 were waited for; matrix products, arithmetic and copies ran while one was open for 0% of the time, Pallas kernels for 6%

profile of v2, /device:TPU:1, one launch (start us, length us, event | category | flops | bytes accessed | tf_op | source)
XLA Modules:
  0.0 117.9 jit_solution(16190577508106264521)
XLA Ops:
  0.6 3.7 %gate_and_turn.1 = bf16[32,48,512]{2,1,0:T(8,128)(2,1)} custom-call(bf16[512,512]{1,0:T(8,128)(2,1)} %bitcast.12, bf16[512,512]{1,0:T(8,128)(2,1)} %bitcast.14, bf16[512,512]{1,0:T(8,128)(2,1)} %bitcast.16, bf16[512,512]{1,0:T(8,128)(2,1)} %bitcast.18, bf16[512,512]{1,0:T(8,128)(2,1)} %refs_4_.1), custom_call_target="tpu_custom_call" | custom-call | flops 201326592 | bytes 4194304 | tf_op jit(solution)/shard_map/gate_and_turn/pallas_call | solution.py:269
  4.3 0.0 copy-start.5
  4.3 0.0 copy-start.6
  4.3 31.5 %all_to_all.15.in_ref = bf16[32,48,512]{2,1,0:T(8,128)(2,1)S(1)} all-to-all(bf16[32,48,512]{2,1,0:T(8,128)(2,1)} %gate_and_turn.1), channel_id=1, replica_groups=mesh['dp'=2,'context'=32,'tensor'=4] {'context'}, dimensions={0} | all-to-all | bytes 3145728 | tf_op jit(solution)/shard_map/all_to_all | solution.py:282
  35.8 0.0 copy-done.5
  35.8 0.0 copy-done.6
  35.8 0.0 copy-start.2
  35.8 0.0 copy-start.3
  35.9 6.2 %transform.1 = (bf16[32,16,512]{2,1,0:T(8,128)(2,1)}, bf16[32,16,512]{2,1,0:T(8,128)(2,1)S(1)}, bf16[32,16,512]{2,1,0:T(8,128)(2,1)S(1)}) custom-call(bf16[32,48,512]{2,1,0:T(8,128)(2,1)S(1)} %all_to_all.15.in_ref, bf16[896,256]{1,0:T(8,128)(2,1)S(1)} %copy-done.5, f32[4,128,128]{2,1,0:T(8,128)S(1)} %copy-done.6), custom_call_target="tpu_custom_call" | custom-call | flops 805306368 | bytes 8388608 | tf_op jit(solution)/shard_map/transform/pallas_call | solution.py:289
  42.0 0.0 copy-start.7
  42.0 0.8 copy-done.7
  42.8 4.0 %all-to-all-start.1 = ((bf16[32,16,512]{2,1,0:T(8,128)(2,1)}), bf16[32,16,512]{2,1,0:T(8,128)(2,1)S(1)}, u32[]{:S(2)}, u32[]{:S(2)}) async-start(bf16[32,16,512]{2,1,0:T(8,128)(2,1)} %get-tuple-element.20), calls=%async_computation.1 | async-start | bytes 1048576 | tf_op jit(solution)/shard_map/all_to_all | solution.py:305
  46.9 7.0 %collective-permute-start.3 = (bf16[32,16,512]{2,1,0:T(8,128)(2,1)S(1)}, bf16[32,16,512]{2,1,0:T(8,128)(2,1)S(1)}, u32[]{:S(2)}, u32[]{:S(2)}) collective-permute-start(bf16[32,16,512]{2,1,0:T(8,128)(2,1)S(1)} %get-tuple-element.24.refs_0_), channel_id=1, source_target_pairs={{0,128},{128,0},{1,129},{129,1},{2,130},{130,2},{3,131},{131,3},{4... | collective-permute-start | bytes 1572872 | tf_op jit(solution)/shard_map/ppermute | solution.py:306
  53.9 0.1 pad_add_fusion.order_ref
  53.9 4.6 %all-to-all-done.1.conv_ref = bf16[32,16,512]{2,1,0:T(8,128)(2,1)S(1)} async-done(((bf16[32,16,512]{2,1,0:T(8,128)(2,1)}), bf16[32,16,512]{2,1,0:T(8,128)(2,1)S(1)}, u32[]{:S(2)}, u32[]{:S(2)}) %all-to-all-start.1) | async-done | bytes 524320 | tf_op jit(solution)/shard_map/all_to_all | solution.py:305
  58.5 0.0 copy-done.2
  58.5 0.0 copy-done.3
  58.5 0.0 copy-start.4
  58.5 1.6 %copy-done.4 = bf16[512,2048]{1,0:T(8,128)(2,1)S(1)} copy-done((bf16[512,2048]{1,0:T(8,128)(2,1)S(1)}, bf16[512,2048]{1,0:T(8,128)(2,1)}, u32[]{:S(2)}) %copy-start.4) | copy-done | bytes 2097176
  60.1 2.9 %project.1 = (bf16[512,512]{1,0:T(8,128)(2,1)S(1)}, bf16[512,512]{1,0:T(8,128)(2,1)}, bf16[512,512]{1,0:T(8,128)(2,1)}, bf16[512,512]{1,0:T(8,128)(2,1)S(1)}, bf16[512,512]{1,0:T(8,128)(2,1)}) custom-call(s32[4]{0:T(128)S(1)} %pad_add_fusion.order_ref, bf16[32,16,512]{2,1,0:T(8,128)(2,1)S(1)} %all-to-all-done.1.conv_ref, bf16[512,512]{1,0:T(8,128)(2,1)S(1)} %bitcast.17, ...), custom_call_target="tpu_custom_call" | custom-call | flops 1073741824 | bytes 6291456 | tf_op jit(solution)/shard_map/project/pallas_call | solution.py:327
  63.0 3.6 %collective-permute-start.4 = (bf16[512,512]{1,0:T(8,128)(2,1)S(1)}, bf16[512,512]{1,0:T(8,128)(2,1)S(1)}, u32[]{:S(2)}, u32[]{:S(2)}) collective-permute-start(bf16[512,512]{1,0:T(8,128)(2,1)S(1)} %get-tuple-element.25.refs_0_), channel_id=1, source_target_pairs={{0,1},{3,2},{4,5},{7,6},{8,9},{11,10},{12,13},{15,14},{16,17},{19,... | collective-permute-start | bytes 1572872 | tf_op jit(solution)/shard_map/ppermute | solution.py:336
  66.6 1.5 %collective-permute-start = (bf16[512,512]{1,0:T(8,128)(2,1)}, bf16[512,512]{1,0:T(8,128)(2,1)}, u32[]{:S(2)}, u32[]{:S(2)}) collective-permute-start(bf16[512,512]{1,0:T(8,128)(2,1)} %get-tuple-element.22), channel_id=1, source_target_pairs={{1,2},{2,1},{5,6},{6,5},{9,10},{10,9},{13,14},{14,13},{17,18},{18,... | collective-permute-start | bytes 1572872 | tf_op jit(solution)/shard_map/ppermute | solution.py:337
  68.0 4.1 %collective-permute-start.2 = (bf16[512,512]{1,0:T(8,128)(2,1)}, bf16[512,512]{1,0:T(8,128)(2,1)}, u32[]{:S(2)}, u32[]{:S(2)}) collective-permute-start(bf16[512,512]{1,0:T(8,128)(2,1)} %get-tuple-element.22), channel_id=1, source_target_pairs={{0,1},{3,2},{4,5},{7,6},{8,9},{11,10},{12,13},{15,14},{16,17},{19,... | collective-permute-start | bytes 1572872 | tf_op jit(solution)/shard_map/ppermute | solution.py:339
  72.2 0.0 collective-permute-start.1
  72.2 0.0 collective-permute-done.3.refs_1_
  72.2 0.1 sum_terms.1.lower_ref
  72.3 0.0 copy-start.8
  72.3 14.4 %collective-permute-done.4.refs_1_ = bf16[512,512]{1,0:T(8,128)(2,1)S(1)} collective-permute-done((bf16[512,512]{1,0:T(8,128)(2,1)S(1)}, bf16[512,512]{1,0:T(8,128)(2,1)S(1)}, u32[]{:S(2)}, u32[]{:S(2)}) %collective-permute-start.4) | collective-permute-done | bytes 524320 | tf_op jit(solution)/shard_map/ppermute | solution.py:336
  86.7 0.1 relay.1
  86.8 1.3 %collective-permute-start.5 = (bf16[512,512]{1,0:T(8,128)(2,1)S(1)}, bf16[512,512]{1,0:T(8,128)(2,1)S(1)}, u32[]{:S(2)}, u32[]{:S(2)}) collective-permute-start(bf16[512,512]{1,0:T(8,128)(2,1)S(1)} %relay.1), channel_id=1, source_target_pairs={{1,3},{2,0},{5,7},{6,4},{9,11},{10,8},{13,15},{14,12},{17,19},{18,... | collective-permute-start | bytes 1572872 | tf_op jit(solution)/shard_map/ppermute | solution.py:344
  88.1 0.0 copy-done.8
  88.1 1.0 join.1
  89.1 9.1 %all-to-all-start.2 = ((bf16[32,32,512]{2,1,0:T(8,128)(2,1)}), bf16[32,32,512]{2,1,0:T(8,128)(2,1)S(1)}, u32[]{:S(2)}, u32[]{:S(2)}) async-start(bf16[32,32,512]{2,1,0:T(8,128)(2,1)} %join.1), calls=%async_computation.2 | async-start | bytes 2097152 | tf_op jit(solution)/shard_map/all_to_all | solution.py:357
  98.3 0.0 collective-permute-done.refs_1_
  98.3 11.0 %collective-permute-done.1.refs_2_ = bf16[512,512]{1,0:T(8,128)(2,1)} collective-permute-done((bf16[512,512]{1,0:T(8,128)(2,1)}, bf16[512,512]{1,0:T(8,128)(2,1)}, u32[]{:S(2)}, u32[]{:S(2)}) %collective-permute-start.1) | collective-permute-done | bytes 524320 | tf_op jit(solution)/shard_map/ppermute | solution.py:338
  109.3 0.0 collective-permute-done.2.refs_3_
  109.3 3.1 %collective-permute-done.5.refs_4_ = bf16[512,512]{1,0:T(8,128)(2,1)S(1)} collective-permute-done((bf16[512,512]{1,0:T(8,128)(2,1)S(1)}, bf16[512,512]{1,0:T(8,128)(2,1)S(1)}, u32[]{:S(2)}, u32[]{:S(2)}) %collective-permute-start.5) | collective-permute-done | bytes 524320 | tf_op jit(solution)/shard_map/ppermute | solution.py:344
  112.4 0.0 copy-start
  112.4 0.0 copy-start.1
  112.4 2.6 %add_parts.1 = bf16[512,512]{1,0:T(8,128)(2,1)} custom-call(bf16[512,512]{1,0:T(8,128)(2,1)S(1)} %get-tuple-element.21.refs_0_, bf16[512,512]{1,0:T(8,128)(2,1)} %collective-permute-done.refs_1_, bf16[512,512]{1,0:T(8,128)(2,1)} %collective-permute-done.1.refs_2_, bf16[512,512]{1,0:T(8,128)(2,1)} %collective-permute-done.2.refs_3_, ...), custom_call_target="tpu_custom_call" | custom-call | flops 99999997952 | bytes 3145728 | tf_op jit(solution)/shard_map/add_parts/pallas_call | solution.py:245
  115.0 0.5 all-to-all-done.2.in_ref
  115.4 0.0 copy-done
  115.4 0.0 copy-done.1
  115.4 2.4 %finish.1 = (bf16[512,512]{1,0:T(8,128)(2,1)}, bf16[512,512]{1,0:T(8,128)(2,1)}, f32[512,512]{1,0:T(8,128)}) custom-call(bf16[32,32,512]{2,1,0:T(8,128)(2,1)S(1)} %all-to-all-done.2.in_ref, bf16[512,512]{1,0:T(8,128)(2,1)S(1)} %bitcast.15, bf16[512,512]{1,0:T(8,128)(2,1)S(1)} %bitcast.13), custom_call_target="tpu_custom_call" | custom-call | flops 134217728 | bytes 2621440 | tf_op jit(solution)/shard_map/finish/pallas_call | solution.py:359
Async XLA Ops:
  4.3 31.5 %copy-start.5 = (bf16[896,256]{1,0:T(8,128)(2,1)S(1)}, bf16[896,256]{1,0:T(8,128)(2,1)}, u32[]{:S(2)}) copy-start(bf16[896,256]{1,0:T(8,128)(2,1)} %constant.16.clone.factors_ref) | copy-start | bytes 1376260
  4.3 31.5 %copy-start.6 = (f32[4,128,128]{2,1,0:T(8,128)S(1)}, f32[4,128,128]{2,1,0:T(8,128)}, u32[]{:S(2)}) copy-start(f32[4,128,128]{2,1,0:T(8,128)} %constant.17.clone.turn) | copy-start | bytes 786436
  35.8 22.7 %copy-start.2 = (bf16[1,512,512]{2,1,0:T(8,128)(2,1)S(1)}, bf16[1,512,512]{2,1,0:T(8,128)(2,1)}, u32[]{:S(2)}) copy-start(bf16[1,512,512]{2,1,0:T(8,128)(2,1)} %param.10) | copy-start | bytes 1572868
  35.8 22.7 %copy-start.3 = (bf16[1,512,512]{2,1,0:T(8,128)(2,1)S(1)}, bf16[1,512,512]{2,1,0:T(8,128)(2,1)}, u32[]{:S(2)}) copy-start(bf16[1,512,512]{2,1,0:T(8,128)(2,1)} %param.13) | copy-start | bytes 1572868
  42.0 0.8 copy-start.7
  42.8 15.7 %all-to-all-start.1 = ((bf16[32,16,512]{2,1,0:T(8,128)(2,1)}), bf16[32,16,512]{2,1,0:T(8,128)(2,1)S(1)}, u32[]{:S(2)}, u32[]{:S(2)}) async-start(bf16[32,16,512]{2,1,0:T(8,128)(2,1)} %get-tuple-element.20), calls=%async_computation.1 | async-start | bytes 1048576 | tf_op jit(solution)/shard_map/all_to_all | solution.py:305
  46.9 25.3 %collective-permute-start.3 = (bf16[32,16,512]{2,1,0:T(8,128)(2,1)S(1)}, bf16[32,16,512]{2,1,0:T(8,128)(2,1)S(1)}, u32[]{:S(2)}, u32[]{:S(2)}) collective-permute-start(bf16[32,16,512]{2,1,0:T(8,128)(2,1)S(1)} %get-tuple-element.24.refs_0_), channel_id=1, source_target_pairs={{0,128},{128,0},{1,129},{129,1},{2,130},{130,2},{3,131},{131,3},{4... | collective-permute-start | bytes 1572872 | tf_op jit(solution)/shard_map/ppermute | solution.py:306
  58.5 1.6 %copy-start.4 = (bf16[512,2048]{1,0:T(8,128)(2,1)S(1)}, bf16[512,2048]{1,0:T(8,128)(2,1)}, u32[]{:S(2)}) copy-start(bf16[512,2048]{1,0:T(8,128)(2,1)} %weight_ref.1) | copy-start | bytes 6291460
  63.0 23.7 %collective-permute-start.4 = (bf16[512,512]{1,0:T(8,128)(2,1)S(1)}, bf16[512,512]{1,0:T(8,128)(2,1)S(1)}, u32[]{:S(2)}, u32[]{:S(2)}) collective-permute-start(bf16[512,512]{1,0:T(8,128)(2,1)S(1)} %get-tuple-element.25.refs_0_), channel_id=1, source_target_pairs={{0,1},{3,2},{4,5},{7,6},{8,9},{11,10},{12,13},{15,14},{16,17},{19,... | collective-permute-start | bytes 1572872 | tf_op jit(solution)/shard_map/ppermute | solution.py:336
  66.6 31.7 %collective-permute-start = (bf16[512,512]{1,0:T(8,128)(2,1)}, bf16[512,512]{1,0:T(8,128)(2,1)}, u32[]{:S(2)}, u32[]{:S(2)}) collective-permute-start(bf16[512,512]{1,0:T(8,128)(2,1)} %get-tuple-element.22), channel_id=1, source_target_pairs={{1,2},{2,1},{5,6},{6,5},{9,10},{10,9},{13,14},{14,13},{17,18},{18,... | collective-permute-start | bytes 1572872 | tf_op jit(solution)/shard_map/ppermute | solution.py:337
  68.0 41.2 %collective-permute-start.2 = (bf16[512,512]{1,0:T(8,128)(2,1)}, bf16[512,512]{1,0:T(8,128)(2,1)}, u32[]{:S(2)}, u32[]{:S(2)}) collective-permute-start(bf16[512,512]{1,0:T(8,128)(2,1)} %get-tuple-element.22), channel_id=1, source_target_pairs={{0,1},{3,2},{4,5},{7,6},{8,9},{11,10},{12,13},{15,14},{16,17},{19,... | collective-permute-start | bytes 1572872 | tf_op jit(solution)/shard_map/ppermute | solution.py:339
  72.2 37.1 %collective-permute-start.1 = (bf16[512,512]{1,0:T(8,128)(2,1)}, bf16[512,512]{1,0:T(8,128)(2,1)}, u32[]{:S(2)}, u32[]{:S(2)}) collective-permute-start(bf16[512,512]{1,0:T(8,128)(2,1)} %get-tuple-element.23), channel_id=1, source_target_pairs={{0,2},{3,1},{1,0},{2,3},{4,6},{7,5},{5,4},{6,7},{8,10},{11,9},{9,8... | collective-permute-start | bytes 1572872 | tf_op jit(solution)/shard_map/ppermute | solution.py:338
  72.3 15.8 %copy-start.8 = (bf16[32,16,512]{2,1,0:T(8,128)(2,1)S(1)}, bf16[32,16,512]{2,1,0:T(8,128)(2,1)}, u32[]{:S(2)}) copy-start(bf16[32,16,512]{2,1,0:T(8,128)(2,1)} %copy-done.7) | copy-start | bytes 1572868
  86.8 25.6 %collective-permute-start.5 = (bf16[512,512]{1,0:T(8,128)(2,1)S(1)}, bf16[512,512]{1,0:T(8,128)(2,1)S(1)}, u32[]{:S(2)}, u32[]{:S(2)}) collective-permute-start(bf16[512,512]{1,0:T(8,128)(2,1)S(1)} %relay.1), channel_id=1, source_target_pairs={{1,3},{2,0},{5,7},{6,4},{9,11},{10,8},{13,15},{14,12},{17,19},{18,... | collective-permute-start | bytes 1572872 | tf_op jit(solution)/shard_map/ppermute | solution.py:344
  89.1 26.3 %all-to-all-start.2 = ((bf16[32,32,512]{2,1,0:T(8,128)(2,1)}), bf16[32,32,512]{2,1,0:T(8,128)(2,1)S(1)}, u32[]{:S(2)}, u32[]{:S(2)}) async-start(bf16[32,32,512]{2,1,0:T(8,128)(2,1)} %join.1), calls=%async_computation.2 | async-start | bytes 2097152 | tf_op jit(solution)/shard_map/all_to_all | solution.py:357
  112.4 3.0 %copy-start = (bf16[1,512,512]{2,1,0:T(8,128)(2,1)S(1)}, bf16[1,512,512]{2,1,0:T(8,128)(2,1)}, u32[]{:S(2)}) copy-start(bf16[1,512,512]{2,1,0:T(8,128)(2,1)} %param.8) | copy-start | bytes 1572868
  112.4 3.0 %copy-start.1 = (bf16[1,512,512]{2,1,0:T(8,128)(2,1)S(1)}, bf16[1,512,512]{2,1,0:T(8,128)(2,1)}, u32[]{:S(2)}) copy-start(bf16[1,512,512]{2,1,0:T(8,128)(2,1)} %param.9) | copy-start | bytes 1572868

commit v3 on v2

--- a/solution.py
+++ b/solution.py
@@ -199,10 +199,10 @@
     refs[-1][...] = total.astype(BF16)
 
 
-def join_kernel(upper_ref, lower_ref, out_ref):
-    group = upper_ref.shape[1]
-    out_ref[:, :group, :] = upper_ref[...]
-    out_ref[:, group:, :] = lower_ref[...]
+def join_kernel(grad_ref, mine_ref, other_ref, out_ref):
+    group = grad_ref.shape[1]
+    out_ref[:, :group, :] = grad_ref[...]
+    out_ref[:, group:, :] = (mine_ref[...].astype(F32) + other_ref[...].astype(F32)).astype(BF16)
 
 
 def project_kernel(order_ref, conv_ref, query_ref, cot_ref, weight_ref, *out_refs):
@@ -316,8 +316,8 @@
     order = jnp.stack(
         [
             toward(3),
-            jnp.where(outer, toward(1), toward(2)),
-            jnp.where(outer, toward(2), toward(0)),
+            toward(2),
+            jnp.where(outer, toward(1), toward(0)),
             at,
         ]
     )
@@ -335,24 +335,21 @@
     )(order, conv_back, query_in, cotangent, out_weight)
     relayed = lax.ppermute(far, "tensor", [(0, 1), (3, 2)])
     across = lax.ppermute(near, "tensor", [(1, 2), (2, 1)])
-    beside = lax.ppermute(other, "tensor", [(0, 2), (3, 1), (1, 0), (2, 3)])
-    inward = lax.ppermute(near, "tensor", [(0, 1), (3, 2)])
-    terms_sum = add_arrays((terms, others), 2 * 10**9, "sum_terms")
-    terms_sum, relayed = lax.optimization_barrier((terms_sum, relayed))
+    beyond = lax.ppermute(near, "tensor", [(0, 2), (3, 1)])
+    beside = lax.ppermute(other, "tensor", [(0, 1), (3, 2), (1, 0), (2, 3)])
     both = add_arrays((far, relayed), 10**11, "relay")
-    terms_sum, both = lax.optimization_barrier((terms_sum, both))
     outward = lax.ppermute(both, "tensor", [(1, 3), (2, 0)])
     joined = pl.pallas_call(
         join_kernel,
-        in_specs=[VMEM] * 2,
+        in_specs=[VMEM] * 3,
         out_specs=VMEM,
         out_shape=jax.ShapeDtypeStruct((sources, 2 * group, block), BF16),
         compiler_params=params(SMALL),
-        cost_estimate=cost(10**11, 4 * 2 * block * chans),
+        cost_estimate=cost(2 * 10**9, 5 * 2 * block * chans),
         name="join",
-    )(grad, terms_sum)
+    )(grad, terms, others)
     mixed_out = add_arrays(
-        (own, across, beside, inward, outward), 10**11, "add_parts"
+        (own, across, beyond, beside, outward), 10**11, "add_parts"
     )
     grads_back = lax.all_to_all(joined, "context", 0, 0, tiled=True)
     scale = 1.0 / math.sqrt(lax.axis_size("dp") * length)

time: 119 us -> 115 us (0.966)
  waiting for transfers between devices: 33.6 us -> 24.1 us
  Pallas kernels: 19 us -> 21.9 us
  starting transfers between devices: 30.5 us -> 32.9 us
    ppermute x1, waiting for transfers between devices: 14.4 us -> 0.93 us  [shards(): relayed = lax.ppermute(far, 'tensor', [(0, 1), (3, 2)])]
    all_to_all x1, waiting for transfers between devices: 0.47 us -> 12.8 us  [shards(): grads_back = lax.all_to_all(joined, 'context', 0, 0, tiled=True)]
    ppermute x2, waiting for transfers between devices: 11 us -> 3.74 us  [the longest x1 3.74 us: shards(): beside = lax.ppermute(other, 'tensor', [(0, 1), (3, 2), (1, 0), (2, 3)])]
    all_to_all x1, starting transfers between devices: 9.12 us -> 11.9 us  [shards(): grads_back = lax.all_to_all(joined, 'context', 0, 0, tiled=True)]
    pallas_call x3 -> x2, Pallas kernels: 2.81 us -> 4.74 us  [add_arrays(): pl.pallas_call(add_kernel, in_specs=[VMEM] * len(arrays), out_specs=VMEM,...]
    unnamed x18 -> x22, local copies, waits for them, and re-layouts: 2.42 us -> 3.22 us
  transfers between devices with their start and end apart: 8 -> 8, of which waited for: 5 -> 5; matrix products, arithmetic and copies ran while one was open for 0% -> 0% of each run, Pallas kernels for 6% -> 8%
where the time goes in v3:
time: 115 us
  starting transfers between devices  32.9 us (29%)
  blocking collectives  31.5 us (27%)
  waiting for transfers between devices  24.1 us (21%)
  Pallas kernels  21.9 us (19%)
  local copies, waits for them, and re-layouts  3.22 us (3%)
    all_to_all x1, blocking collectives, shards(): received = lax.all_to_all(sent, 'context', 0, 0, tiled=True)  31.5 us
    all_to_all x1, waiting for transfers between devices, shards(): grads_back = lax.all_to_all(joined, 'context', 0, 0, tiled=True)  12.8 us
    all_to_all x1, starting transfers between devices, shards(): grads_back = lax.all_to_all(joined, 'context', 0, 0, tiled=True)  11.9 us
    ppermute x1, starting transfers between devices, shards(): others = lax.ppermute(terms, 'dp', [(0, 1), (1, 0)])  7.01 us
    pallas_call x1, Pallas kernels, shards(): pl.pallas_call(transform_kernel, in_specs=[VMEM] * 3, out_specs=[VMEM] *...  6.19 us
    pallas_call x2, Pallas kernels, add_arrays(): pl.pallas_call(add_kernel, in_specs=[VMEM] * len(arrays), out_specs=VMEM,...  4.74 us
    all_to_all x1, waiting for transfers between devices, shards(): conv_back = lax.all_to_all(conv, 'context', 0, 0, tiled=True)  4.68 us
    ppermute x1, starting transfers between devices, shards(): relayed = lax.ppermute(far, 'tensor', [(0, 1), (3, 2)])  4.36 us
  transfers between devices with their start and end apart: 8, of which 5 were waited for; matrix products, arithmetic and copies ran while one was open for 0% of the time, Pallas kernels for 8%

profile of v3, /device:TPU:1, one launch (start us, length us, event | category | flops | bytes accessed | tf_op | source)
XLA Modules:
  0.0 114.5 jit_solution(11013742953656497554)
XLA Ops:
  0.6 3.7 %gate_and_turn.1 = bf16[32,48,512]{2,1,0:T(8,128)(2,1)} custom-call(bf16[512,512]{1,0:T(8,128)(2,1)} %bitcast.12, bf16[512,512]{1,0:T(8,128)(2,1)} %bitcast.14, bf16[512,512]{1,0:T(8,128)(2,1)} %bitcast.16, bf16[512,512]{1,0:T(8,128)(2,1)} %bitcast.18, bf16[512,512]{1,0:T(8,128)(2,1)} %refs_4_.1), custom_call_target="tpu_custom_call" | custom-call | flops 201326592 | bytes 4194304 | tf_op jit(solution)/shard_map/gate_and_turn/pallas_call | solution.py:269
  4.3 0.0 copy-start.5
  4.3 0.0 copy-start.6
  4.3 31.5 %all_to_all.15.in_ref = bf16[32,48,512]{2,1,0:T(8,128)(2,1)S(1)} all-to-all(bf16[32,48,512]{2,1,0:T(8,128)(2,1)} %gate_and_turn.1), channel_id=1, replica_groups=mesh['dp'=2,'context'=32,'tensor'=4] {'context'}, dimensions={0} | all-to-all | bytes 3145728 | tf_op jit(solution)/shard_map/all_to_all | solution.py:282
  35.8 0.0 copy-done.5
  35.8 0.0 copy-done.6
  35.8 0.0 copy-start.2
  35.8 0.0 copy-start.3
  35.8 6.2 %transform.1 = (bf16[32,16,512]{2,1,0:T(8,128)(2,1)}, bf16[32,16,512]{2,1,0:T(8,128)(2,1)S(1)}, bf16[32,16,512]{2,1,0:T(8,128)(2,1)S(1)}) custom-call(bf16[32,48,512]{2,1,0:T(8,128)(2,1)S(1)} %all_to_all.15.in_ref, bf16[896,256]{1,0:T(8,128)(2,1)S(1)} %copy-done.5, f32[4,128,128]{2,1,0:T(8,128)S(1)} %copy-done.6), custom_call_target="tpu_custom_call" | custom-call | flops 805306368 | bytes 8388608 | tf_op jit(solution)/shard_map/transform/pallas_call | solution.py:289
  42.0 0.0 copy-start.9
  42.0 0.8 copy-done.9
  42.8 4.0 %all-to-all-start.1 = ((bf16[32,16,512]{2,1,0:T(8,128)(2,1)}), bf16[32,16,512]{2,1,0:T(8,128)(2,1)S(1)}, u32[]{:S(2)}, u32[]{:S(2)}) async-start(bf16[32,16,512]{2,1,0:T(8,128)(2,1)} %get-tuple-element.16), calls=%async_computation.1 | async-start | bytes 1048576 | tf_op jit(solution)/shard_map/all_to_all | solution.py:305
  46.8 7.0 %collective-permute-start.5 = (bf16[32,16,512]{2,1,0:T(8,128)(2,1)S(1)}, bf16[32,16,512]{2,1,0:T(8,128)(2,1)}, u32[]{:S(2)}, u32[]{:S(2)}) collective-permute-start(bf16[32,16,512]{2,1,0:T(8,128)(2,1)S(1)} %get-tuple-element.22.mine_ref), channel_id=1, source_target_pairs={{0,128},{128,0},{1,129},{129,1},{2,130},{130,2},{3,131},{131,3},{4... | collective-permute-start | bytes 1572872 | tf_op jit(solution)/shard_map/ppermute | solution.py:306
  53.9 0.1 pad_add_fusion.order_ref
  53.9 4.7 %all-to-all-done.1.conv_ref = bf16[32,16,512]{2,1,0:T(8,128)(2,1)S(1)} async-done(((bf16[32,16,512]{2,1,0:T(8,128)(2,1)}), bf16[32,16,512]{2,1,0:T(8,128)(2,1)S(1)}, u32[]{:S(2)}, u32[]{:S(2)}) %all-to-all-start.1) | async-done | bytes 524320 | tf_op jit(solution)/shard_map/all_to_all | solution.py:305
  58.6 0.0 copy-done.2
  58.6 0.0 copy-done.3
  58.6 0.0 copy-start.4
  58.6 1.6 %copy-done.4 = bf16[512,2048]{1,0:T(8,128)(2,1)S(1)} copy-done((bf16[512,2048]{1,0:T(8,128)(2,1)S(1)}, bf16[512,2048]{1,0:T(8,128)(2,1)}, u32[]{:S(2)}) %copy-start.4) | copy-done | bytes 2097176
  60.2 0.0 copy-start.10
  60.2 2.7 %project.1 = (bf16[512,512]{1,0:T(8,128)(2,1)}, bf16[512,512]{1,0:T(8,128)(2,1)S(1)}, bf16[512,512]{1,0:T(8,128)(2,1)S(1)}, bf16[512,512]{1,0:T(8,128)(2,1)S(1)}, bf16[512,512]{1,0:T(8,128)(2,1)}) custom-call(s32[4]{0:T(128)S(1)} %pad_add_fusion.order_ref, bf16[32,16,512]{2,1,0:T(8,128)(2,1)S(1)} %all-to-all-done.1.conv_ref, bf16[512,512]{1,0:T(8,128)(2,1)S(1)} %bitcast.17, ...), custom_call_target="tpu_custom_call" | custom-call | flops 1073741824 | bytes 6291456 | tf_op jit(solution)/shard_map/project/pallas_call | solution.py:327
  62.9 0.0 copy-start.7
  62.9 0.8 copy-done.7
  63.7 4.4 %collective-permute-start.3 = (bf16[512,512]{1,0:T(8,128)(2,1)}, bf16[512,512]{1,0:T(8,128)(2,1)}, u32[]{:S(2)}, u32[]{:S(2)}) collective-permute-start(bf16[512,512]{1,0:T(8,128)(2,1)} %get-tuple-element.20.refs_0_), channel_id=1, source_target_pairs={{0,1},{3,2},{4,5},{7,6},{8,9},{11,10},{12,13},{15,14},{16,17},{19,... | collective-permute-start | bytes 1572872 | tf_op jit(solution)/shard_map/ppermute | solution.py:336
  68.1 1.5 %collective-permute-start = (bf16[512,512]{1,0:T(8,128)(2,1)S(1)}, bf16[512,512]{1,0:T(8,128)(2,1)}, u32[]{:S(2)}, u32[]{:S(2)}) collective-permute-start(bf16[512,512]{1,0:T(8,128)(2,1)S(1)} %get-tuple-element.18), channel_id=1, source_target_pairs={{1,2},{2,1},{5,6},{6,5},{9,10},{10,9},{13,14},{14,13},{17,18},{18,... | collective-permute-start | bytes 1572872 | tf_op jit(solution)/shard_map/ppermute | solution.py:337
  69.5 2.9 %collective-permute-start.1 = (bf16[512,512]{1,0:T(8,128)(2,1)S(1)}, bf16[512,512]{1,0:T(8,128)(2,1)}, u32[]{:S(2)}, u32[]{:S(2)}) collective-permute-start(bf16[512,512]{1,0:T(8,128)(2,1)S(1)} %get-tuple-element.18), channel_id=1, source_target_pairs={{0,2},{3,1},{4,6},{7,5},{8,10},{11,9},{12,14},{15,13},{16,18},{19,... | collective-permute-start | bytes 1572872 | tf_op jit(solution)/shard_map/ppermute | solution.py:338
  72.5 0.0 collective-permute-start.2
  72.5 0.0 collective-permute-done.5.other_ref
  72.5 0.0 copy-done.10
  72.5 2.2 %join.1 = bf16[32,32,512]{2,1,0:T(8,128)(2,1)} custom-call(bf16[32,16,512]{2,1,0:T(8,128)(2,1)S(1)} %copy-done.10, bf16[32,16,512]{2,1,0:T(8,128)(2,1)S(1)} %get-tuple-element.22.mine_ref, bf16[32,16,512]{2,1,0:T(8,128)(2,1)} %collective-permute-done.5.other_ref), custom_call_target="tpu_custom_call" | custom-call | flops 2000000000 | bytes 2621440 | tf_op jit(solution)/shard_map/join/pallas_call | solution.py:342
  74.7 11.9 %all-to-all-start.2 = ((bf16[32,32,512]{2,1,0:T(8,128)(2,1)}), bf16[32,32,512]{2,1,0:T(8,128)(2,1)S(1)}, u32[]{:S(2)}, u32[]{:S(2)}) async-start(bf16[32,32,512]{2,1,0:T(8,128)(2,1)} %join.1), calls=%async_computation.2 | async-start | bytes 2097152 | tf_op jit(solution)/shard_map/all_to_all | solution.py:354
  86.6 0.0 copy-start
  86.6 0.0 copy-start.1
  86.6 0.9 collective-permute-done.3.refs_1_
  87.5 2.1 %relay.1 = bf16[512,512]{1,0:T(8,128)(2,1)} custom-call(bf16[512,512]{1,0:T(8,128)(2,1)} %get-tuple-element.20.refs_0_, bf16[512,512]{1,0:T(8,128)(2,1)} %collective-permute-done.3.refs_1_), custom_call_target="tpu_custom_call" | custom-call | flops 99999997952 | bytes 1572864 | tf_op jit(solution)/shard_map/relay/pallas_call | solution.py:245
  89.6 1.3 %collective-permute-start.4 = (bf16[512,512]{1,0:T(8,128)(2,1)}, bf16[512,512]{1,0:T(8,128)(2,1)}, u32[]{:S(2)}, u32[]{:S(2)}) collective-permute-start(bf16[512,512]{1,0:T(8,128)(2,1)} %relay.1), channel_id=1, source_target_pairs={{1,3},{2,0},{5,7},{6,4},{9,11},{10,8},{13,15},{14,12},{17,19},{18,... | collective-permute-start | bytes 1572872 | tf_op jit(solution)/shard_map/ppermute | solution.py:341
  90.9 12.8 %all-to-all-done.2.in_ref = bf16[32,32,512]{2,1,0:T(8,128)(2,1)S(1)} async-done(((bf16[32,32,512]{2,1,0:T(8,128)(2,1)}), bf16[32,32,512]{2,1,0:T(8,128)(2,1)S(1)}, u32[]{:S(2)}, u32[]{:S(2)}) %all-to-all-start.2) | async-done | bytes 1048608 | tf_op jit(solution)/shard_map/all_to_all | solution.py:354
  103.7 0.0 copy-done
  103.7 0.0 copy-done.1
  103.7 0.0 copy-start.8
  103.8 2.4 %finish.1 = (bf16[512,512]{1,0:T(8,128)(2,1)}, bf16[512,512]{1,0:T(8,128)(2,1)}, f32[512,512]{1,0:T(8,128)}) custom-call(bf16[32,32,512]{2,1,0:T(8,128)(2,1)S(1)} %all-to-all-done.2.in_ref, bf16[512,512]{1,0:T(8,128)(2,1)S(1)} %bitcast.15, bf16[512,512]{1,0:T(8,128)(2,1)S(1)} %bitcast.13), custom_call_target="tpu_custom_call" | custom-call | flops 134217728 | bytes 2621440 | tf_op jit(solution)/shard_map/finish/pallas_call | solution.py:356
  106.2 0.0 collective-permute-done.refs_1_
  106.2 0.0 collective-permute-done.1.refs_2_
  106.2 3.7 %collective-permute-done.2.refs_3_ = bf16[512,512]{1,0:T(8,128)(2,1)} collective-permute-done((bf16[512,512]{1,0:T(8,128)(2,1)S(1)}, bf16[512,512]{1,0:T(8,128)(2,1)}, u32[]{:S(2)}, u32[]{:S(2)}) %collective-permute-start.2) | collective-permute-done | bytes 524320 | tf_op jit(solution)/shard_map/ppermute | solution.py:339
  109.9 1.9 %collective-permute-done.4.refs_4_ = bf16[512,512]{1,0:T(8,128)(2,1)} collective-permute-done((bf16[512,512]{1,0:T(8,128)(2,1)}, bf16[512,512]{1,0:T(8,128)(2,1)}, u32[]{:S(2)}, u32[]{:S(2)}) %collective-permute-start.4) | collective-permute-done | bytes 524320 | tf_op jit(solution)/shard_map/ppermute | solution.py:341
  111.9 0.0 copy-done.8
  111.9 2.6 %add_parts.1 = bf16[512,512]{1,0:T(8,128)(2,1)} custom-call(bf16[512,512]{1,0:T(8,128)(2,1)S(1)} %copy-done.8, bf16[512,512]{1,0:T(8,128)(2,1)} %collective-permute-done.refs_1_, bf16[512,512]{1,0:T(8,128)(2,1)} %collective-permute-done.1.refs_2_, bf16[512,512]{1,0:T(8,128)(2,1)} %collective-permute-done.2.refs_3_, ...), custom_call_target="tpu_custom_call" | custom-call | flops 99999997952 | bytes 3145728 | tf_op jit(solution)/shard_map/add_parts/pallas_call | solution.py:245
Async XLA Ops:
  4.3 31.5 %copy-start.5 = (bf16[896,256]{1,0:T(8,128)(2,1)S(1)}, bf16[896,256]{1,0:T(8,128)(2,1)}, u32[]{:S(2)}) copy-start(bf16[896,256]{1,0:T(8,128)(2,1)} %constant.16.clone.factors_ref) | copy-start | bytes 1376260
  4.3 31.5 %copy-start.6 = (f32[4,128,128]{2,1,0:T(8,128)S(1)}, f32[4,128,128]{2,1,0:T(8,128)}, u32[]{:S(2)}) copy-start(f32[4,128,128]{2,1,0:T(8,128)} %constant.17.clone.turn) | copy-start | bytes 786436
  35.8 22.8 %copy-start.2 = (bf16[1,512,512]{2,1,0:T(8,128)(2,1)S(1)}, bf16[1,512,512]{2,1,0:T(8,128)(2,1)}, u32[]{:S(2)}) copy-start(bf16[1,512,512]{2,1,0:T(8,128)(2,1)} %param.10) | copy-start | bytes 1572868
  35.8 22.8 %copy-start.3 = (bf16[1,512,512]{2,1,0:T(8,128)(2,1)S(1)}, bf16[1,512,512]{2,1,0:T(8,128)(2,1)}, u32[]{:S(2)}) copy-start(bf16[1,512,512]{2,1,0:T(8,128)(2,1)} %param.13) | copy-start | bytes 1572868
  42.0 0.8 copy-start.9
  42.8 15.8 %all-to-all-start.1 = ((bf16[32,16,512]{2,1,0:T(8,128)(2,1)}), bf16[32,16,512]{2,1,0:T(8,128)(2,1)S(1)}, u32[]{:S(2)}, u32[]{:S(2)}) async-start(bf16[32,16,512]{2,1,0:T(8,128)(2,1)} %get-tuple-element.16), calls=%async_computation.1 | async-start | bytes 1048576 | tf_op jit(solution)/shard_map/all_to_all | solution.py:305
  46.8 25.6 %collective-permute-start.5 = (bf16[32,16,512]{2,1,0:T(8,128)(2,1)S(1)}, bf16[32,16,512]{2,1,0:T(8,128)(2,1)}, u32[]{:S(2)}, u32[]{:S(2)}) collective-permute-start(bf16[32,16,512]{2,1,0:T(8,128)(2,1)S(1)} %get-tuple-element.22.mine_ref), channel_id=1, source_target_pairs={{0,128},{128,0},{1,129},{129,1},{2,130},{130,2},{3,131},{131,3},{4... | collective-permute-start | bytes 1572872 | tf_op jit(solution)/shard_map/ppermute | solution.py:306
  58.6 1.6 %copy-start.4 = (bf16[512,2048]{1,0:T(8,128)(2,1)S(1)}, bf16[512,2048]{1,0:T(8,128)(2,1)}, u32[]{:S(2)}) copy-start(bf16[512,2048]{1,0:T(8,128)(2,1)} %weight_ref.1) | copy-start | bytes 6291460
  60.2 12.3 %copy-start.10 = (bf16[32,16,512]{2,1,0:T(8,128)(2,1)S(1)}, bf16[32,16,512]{2,1,0:T(8,128)(2,1)}, u32[]{:S(2)}) copy-start(bf16[32,16,512]{2,1,0:T(8,128)(2,1)} %copy-done.9) | copy-start | bytes 1572868
  62.9 0.8 copy-start.7
  63.7 23.8 %collective-permute-start.3 = (bf16[512,512]{1,0:T(8,128)(2,1)}, bf16[512,512]{1,0:T(8,128)(2,1)}, u32[]{:S(2)}, u32[]{:S(2)}) collective-permute-start(bf16[512,512]{1,0:T(8,128)(2,1)} %get-tuple-element.20.refs_0_), channel_id=1, source_target_pairs={{0,1},{3,2},{4,5},{7,6},{8,9},{11,10},{12,13},{15,14},{16,17},{19,... | collective-permute-start | bytes 1572872 | tf_op jit(solution)/shard_map/ppermute | solution.py:336
  68.1 38.1 %collective-permute-start = (bf16[512,512]{1,0:T(8,128)(2,1)S(1)}, bf16[512,512]{1,0:T(8,128)(2,1)}, u32[]{:S(2)}, u32[]{:S(2)}) collective-permute-start(bf16[512,512]{1,0:T(8,128)(2,1)S(1)} %get-tuple-element.18), channel_id=1, source_target_pairs={{1,2},{2,1},{5,6},{6,5},{9,10},{10,9},{13,14},{14,13},{17,18},{18,... | collective-permute-start | bytes 1572872 | tf_op jit(solution)/shard_map/ppermute | solution.py:337
  69.5 36.6 %collective-permute-start.1 = (bf16[512,512]{1,0:T(8,128)(2,1)S(1)}, bf16[512,512]{1,0:T(8,128)(2,1)}, u32[]{:S(2)}, u32[]{:S(2)}) collective-permute-start(bf16[512,512]{1,0:T(8,128)(2,1)S(1)} %get-tuple-element.18), channel_id=1, source_target_pairs={{0,2},{3,1},{4,6},{7,5},{8,10},{11,9},{12,14},{15,13},{16,18},{19,... | collective-permute-start | bytes 1572872 | tf_op jit(solution)/shard_map/ppermute | solution.py:338
  72.5 37.4 %collective-permute-start.2 = (bf16[512,512]{1,0:T(8,128)(2,1)S(1)}, bf16[512,512]{1,0:T(8,128)(2,1)}, u32[]{:S(2)}, u32[]{:S(2)}) collective-permute-start(bf16[512,512]{1,0:T(8,128)(2,1)S(1)} %get-tuple-element.19), channel_id=1, source_target_pairs={{0,1},{3,2},{1,0},{2,3},{4,5},{7,6},{5,4},{6,7},{8,9},{11,10},{9,8... | collective-permute-start | bytes 1572872 | tf_op jit(solution)/shard_map/ppermute | solution.py:339
  74.7 29.1 %all-to-all-start.2 = ((bf16[32,32,512]{2,1,0:T(8,128)(2,1)}), bf16[32,32,512]{2,1,0:T(8,128)(2,1)S(1)}, u32[]{:S(2)}, u32[]{:S(2)}) async-start(bf16[32,32,512]{2,1,0:T(8,128)(2,1)} %join.1), calls=%async_computation.2 | async-start | bytes 2097152 | tf_op jit(solution)/shard_map/all_to_all | solution.py:354
  86.6 17.2 %copy-start = (bf16[1,512,512]{2,1,0:T(8,128)(2,1)S(1)}, bf16[1,512,512]{2,1,0:T(8,128)(2,1)}, u32[]{:S(2)}) copy-start(bf16[1,512,512]{2,1,0:T(8,128)(2,1)} %param.8) | copy-start | bytes 1572868
  86.6 17.2 %copy-start.1 = (bf16[1,512,512]{2,1,0:T(8,128)(2,1)S(1)}, bf16[1,512,512]{2,1,0:T(8,128)(2,1)}, u32[]{:S(2)}) copy-start(bf16[1,512,512]{2,1,0:T(8,128)(2,1)} %param.9) | copy-start | bytes 1572868
  89.6 22.2 %collective-permute-start.4 = (bf16[512,512]{1,0:T(8,128)(2,1)}, bf16[512,512]{1,0:T(8,128)(2,1)}, u32[]{:S(2)}, u32[]{:S(2)}) collective-permute-start(bf16[512,512]{1,0:T(8,128)(2,1)} %relay.1), channel_id=1, source_target_pairs={{1,3},{2,0},{5,7},{6,4},{9,11},{10,8},{13,15},{14,12},{17,19},{18,... | collective-permute-start | bytes 1572872 | tf_op jit(solution)/shard_map/ppermute | solution.py:341
  103.7 8.1 %copy-start.8 = (bf16[512,512]{1,0:T(8,128)(2,1)S(1)}, bf16[512,512]{1,0:T(8,128)(2,1)}, u32[]{:S(2)}) copy-start(bf16[512,512]{1,0:T(8,128)(2,1)} %copy-done.7) | copy-start | bytes 1572868

commit v4 on v3

--- a/solution.py
+++ b/solution.py
@@ -68,7 +68,7 @@
 
 
 def gate_kernel(*refs):
-    in_refs, (out_ref, held, arrival) = refs[:5], refs[5:]
+    in_refs, (out_hbm, held, out_ref, arrival, departure) = refs[:5], refs[5:]
     _, chunks, _, width = held.shape
 
     def copy(one, chunk):
@@ -83,6 +83,11 @@
             copy(one, chunk).start()
     group = out_ref.shape[1] // 3
     share = out_ref.shape[0] // chunks
+
+    def send(chunk):
+        part = pl.ds(chunk * share, share)
+        return pltpu.make_async_copy(out_ref.at[part], out_hbm.at[part], departure.at[chunk])
+
     for chunk in range(chunks):
         for one in range(5):
             copy(one, chunk).wait()
@@ -92,6 +97,9 @@
             out_ref[
                 chunk * share : (chunk + 1) * share, slot * group : (slot + 1) * group, :
             ] = turned.reshape(share, group, turned.shape[1])
+        send(chunk).start()
+    for chunk in range(chunks):
+        send(chunk).wait()
 
 
 def spread(in_ref, first_row, wide_ref, group):
@@ -269,11 +277,13 @@
     sent = pl.pallas_call(
         gate_kernel,
         in_specs=[HBM] * 5,
-        out_specs=VMEM,
+        out_specs=HBM,
         out_shape=jax.ShapeDtypeStruct((sources, 3 * group, block), BF16),
         scratch_shapes=[
             pltpu.VMEM((5, steps, block, LANES), BF16),
+            pltpu.VMEM((sources, 3 * group, block), BF16),
             pltpu.SemaphoreType.DMA((5, steps)),
+            pltpu.SemaphoreType.DMA((steps,)),
         ],
         compiler_params=params(),
         cost_estimate=cost(6 * block * chans * LANES, 8 * 2 * block * chans),

time: 115 us -> 115 us (level)
  no operation moved by 1% of the time
where the time goes in v4:
time: 115 us; the launch traced here: 114 us
  starting transfers between devices  32.9 us (29%)
  blocking collectives  31.5 us (27%)
  waiting for transfers between devices  24.2 us (21%)
  Pallas kernels  21.5 us (19%)
  local copies, waits for them, and re-layouts  3.22 us (3%)
    all_to_all x1, blocking collectives, shards(): received = lax.all_to_all(sent, 'context', 0, 0, tiled=True)  31.5 us
    all_to_all x1, waiting for transfers between devices, shards(): grads_back = lax.all_to_all(joined, 'context', 0, 0, tiled=True)  12.8 us
    all_to_all x1, starting transfers between devices, shards(): grads_back = lax.all_to_all(joined, 'context', 0, 0, tiled=True)  11.9 us
    ppermute x1, starting transfers between devices, shards(): others = lax.ppermute(terms, 'dp', [(0, 1), (1, 0)])  6.99 us
    pallas_call x1, Pallas kernels, shards(): pl.pallas_call(transform_kernel, in_specs=[VMEM] * 3, out_specs=[VMEM] *...  6.19 us
    pallas_call x2, Pallas kernels, add_arrays(): pl.pallas_call(add_kernel, in_specs=[VMEM] * len(arrays), out_specs=VMEM,...  4.74 us
    all_to_all x1, waiting for transfers between devices, shards(): conv_back = lax.all_to_all(conv, 'context', 0, 0, tiled=True)  4.7 us
    ppermute x1, starting transfers between devices, shards(): relayed = lax.ppermute(far, 'tensor', [(0, 1), (3, 2)])  4.34 us
  transfers between devices with their start and end apart: 8, of which 5 were waited for; matrix products, arithmetic and copies ran while one was open for 0% of the time, Pallas kernels for 8%

profile of v4, /device:TPU:1, one launch (start us, length us, event | category | flops | bytes accessed | tf_op | source)
XLA Modules:
  0.0 114.1 jit_solution(9108604966788803569)
XLA Ops:
  0.6 3.3 %gate_and_turn.1 = bf16[32,48,512]{2,1,0:T(8,128)(2,1)} custom-call(bf16[512,512]{1,0:T(8,128)(2,1)} %bitcast.12, bf16[512,512]{1,0:T(8,128)(2,1)} %bitcast.14, bf16[512,512]{1,0:T(8,128)(2,1)} %bitcast.16, bf16[512,512]{1,0:T(8,128)(2,1)} %bitcast.18, bf16[512,512]{1,0:T(8,128)(2,1)} %refs_4_.1), custom_call_target="tpu_custom_call" | custom-call | flops 201326592 | bytes 4194304 | tf_op jit(solution)/shard_map/gate_and_turn/pallas_call | solution.py:277
  3.9 0.0 copy-start.5
  3.9 0.0 copy-start.6
  3.9 31.5 %all_to_all.15.in_ref = bf16[32,48,512]{2,1,0:T(8,128)(2,1)S(1)} all-to-all(bf16[32,48,512]{2,1,0:T(8,128)(2,1)} %gate_and_turn.1), channel_id=1, replica_groups=mesh['dp'=2,'context'=32,'tensor'=4] {'context'}, dimensions={0} | all-to-all | bytes 3145728 | tf_op jit(solution)/shard_map/all_to_all | solution.py:292
  35.5 0.0 copy-done.5
  35.5 0.0 copy-done.6
  35.5 0.0 copy-start.2
  35.5 0.0 copy-start.3
  35.5 6.2 %transform.1 = (bf16[32,16,512]{2,1,0:T(8,128)(2,1)}, bf16[32,16,512]{2,1,0:T(8,128)(2,1)S(1)}, bf16[32,16,512]{2,1,0:T(8,128)(2,1)S(1)}) custom-call(bf16[32,48,512]{2,1,0:T(8,128)(2,1)S(1)} %all_to_all.15.in_ref, bf16[896,256]{1,0:T(8,128)(2,1)S(1)} %copy-done.5, f32[4,128,128]{2,1,0:T(8,128)S(1)} %copy-done.6), custom_call_target="tpu_custom_call" | custom-call | flops 805306368 | bytes 8388608 | tf_op jit(solution)/shard_map/transform/pallas_call | solution.py:299
  41.7 0.0 copy-start.9
  41.7 0.8 copy-done.9
  42.5 4.0 %all-to-all-start.1 = ((bf16[32,16,512]{2,1,0:T(8,128)(2,1)}), bf16[32,16,512]{2,1,0:T(8,128)(2,1)S(1)}, u32[]{:S(2)}, u32[]{:S(2)}) async-start(bf16[32,16,512]{2,1,0:T(8,128)(2,1)} %get-tuple-element.16), calls=%async_computation.1 | async-start | bytes 1048576 | tf_op jit(solution)/shard_map/all_to_all | solution.py:315
  46.5 7.0 %collective-permute-start.5 = (bf16[32,16,512]{2,1,0:T(8,128)(2,1)S(1)}, bf16[32,16,512]{2,1,0:T(8,128)(2,1)}, u32[]{:S(2)}, u32[]{:S(2)}) collective-permute-start(bf16[32,16,512]{2,1,0:T(8,128)(2,1)S(1)} %get-tuple-element.22.mine_ref), channel_id=1, source_target_pairs={{0,128},{128,0},{1,129},{129,1},{2,130},{130,2},{3,131},{131,3},{4... | collective-permute-start | bytes 1572872 | tf_op jit(solution)/shard_map/ppermute | solution.py:316
  53.5 0.1 pad_add_fusion.order_ref
  53.5 4.7 %all-to-all-done.1.conv_ref = bf16[32,16,512]{2,1,0:T(8,128)(2,1)S(1)} async-done(((bf16[32,16,512]{2,1,0:T(8,128)(2,1)}), bf16[32,16,512]{2,1,0:T(8,128)(2,1)S(1)}, u32[]{:S(2)}, u32[]{:S(2)}) %all-to-all-start.1) | async-done | bytes 524320 | tf_op jit(solution)/shard_map/all_to_all | solution.py:315
  58.2 0.0 copy-done.2
  58.2 0.0 copy-done.3
  58.2 0.0 copy-start.4
  58.3 1.6 %copy-done.4 = bf16[512,2048]{1,0:T(8,128)(2,1)S(1)} copy-done((bf16[512,2048]{1,0:T(8,128)(2,1)S(1)}, bf16[512,2048]{1,0:T(8,128)(2,1)}, u32[]{:S(2)}) %copy-start.4) | copy-done | bytes 2097176
  59.8 0.0 copy-start.10
  59.8 2.7 %project.1 = (bf16[512,512]{1,0:T(8,128)(2,1)}, bf16[512,512]{1,0:T(8,128)(2,1)S(1)}, bf16[512,512]{1,0:T(8,128)(2,1)S(1)}, bf16[512,512]{1,0:T(8,128)(2,1)S(1)}, bf16[512,512]{1,0:T(8,128)(2,1)}) custom-call(s32[4]{0:T(128)S(1)} %pad_add_fusion.order_ref, bf16[32,16,512]{2,1,0:T(8,128)(2,1)S(1)} %all-to-all-done.1.conv_ref, bf16[512,512]{1,0:T(8,128)(2,1)S(1)} %bitcast.17, ...), custom_call_target="tpu_custom_call" | custom-call | flops 1073741824 | bytes 6291456 | tf_op jit(solution)/shard_map/project/pallas_call | solution.py:337
  62.6 0.0 copy-start.7
  62.6 0.8 copy-done.7
  63.4 4.3 %collective-permute-start.3 = (bf16[512,512]{1,0:T(8,128)(2,1)}, bf16[512,512]{1,0:T(8,128)(2,1)}, u32[]{:S(2)}, u32[]{:S(2)}) collective-permute-start(bf16[512,512]{1,0:T(8,128)(2,1)} %get-tuple-element.20.refs_0_), channel_id=1, source_target_pairs={{0,1},{3,2},{4,5},{7,6},{8,9},{11,10},{12,13},{15,14},{16,17},{19,... | collective-permute-start | bytes 1572872 | tf_op jit(solution)/shard_map/ppermute | solution.py:346
  67.7 1.5 %collective-permute-start = (bf16[512,512]{1,0:T(8,128)(2,1)S(1)}, bf16[512,512]{1,0:T(8,128)(2,1)}, u32[]{:S(2)}, u32[]{:S(2)}) collective-permute-start(bf16[512,512]{1,0:T(8,128)(2,1)S(1)} %get-tuple-element.18), channel_id=1, source_target_pairs={{1,2},{2,1},{5,6},{6,5},{9,10},{10,9},{13,14},{14,13},{17,18},{18,... | collective-permute-start | bytes 1572872 | tf_op jit(solution)/shard_map/ppermute | solution.py:347
  69.2 2.9 %collective-permute-start.1 = (bf16[512,512]{1,0:T(8,128)(2,1)S(1)}, bf16[512,512]{1,0:T(8,128)(2,1)}, u32[]{:S(2)}, u32[]{:S(2)}) collective-permute-start(bf16[512,512]{1,0:T(8,128)(2,1)S(1)} %get-tuple-element.18), channel_id=1, source_target_pairs={{0,2},{3,1},{4,6},{7,5},{8,10},{11,9},{12,14},{15,13},{16,18},{19,... | collective-permute-start | bytes 1572872 | tf_op jit(solution)/shard_map/ppermute | solution.py:348
  72.1 0.0 collective-permute-start.2
  72.1 0.0 collective-permute-done.5.other_ref
  72.1 0.0 copy-done.10
  72.1 2.2 %join.1 = bf16[32,32,512]{2,1,0:T(8,128)(2,1)} custom-call(bf16[32,16,512]{2,1,0:T(8,128)(2,1)S(1)} %copy-done.10, bf16[32,16,512]{2,1,0:T(8,128)(2,1)S(1)} %get-tuple-element.22.mine_ref, bf16[32,16,512]{2,1,0:T(8,128)(2,1)} %collective-permute-done.5.other_ref), custom_call_target="tpu_custom_call" | custom-call | flops 2000000000 | bytes 2621440 | tf_op jit(solution)/shard_map/join/pallas_call | solution.py:352
  74.3 11.9 %all-to-all-start.2 = ((bf16[32,32,512]{2,1,0:T(8,128)(2,1)}), bf16[32,32,512]{2,1,0:T(8,128)(2,1)S(1)}, u32[]{:S(2)}, u32[]{:S(2)}) async-start(bf16[32,32,512]{2,1,0:T(8,128)(2,1)} %join.1), calls=%async_computation.2 | async-start | bytes 2097152 | tf_op jit(solution)/shard_map/all_to_all | solution.py:364
  86.2 0.0 copy-start
  86.2 0.0 copy-start.1
  86.2 0.9 collective-permute-done.3.refs_1_
  87.1 2.1 %relay.1 = bf16[512,512]{1,0:T(8,128)(2,1)} custom-call(bf16[512,512]{1,0:T(8,128)(2,1)} %get-tuple-element.20.refs_0_, bf16[512,512]{1,0:T(8,128)(2,1)} %collective-permute-done.3.refs_1_), custom_call_target="tpu_custom_call" | custom-call | flops 99999997952 | bytes 1572864 | tf_op jit(solution)/shard_map/relay/pallas_call | solution.py:253
  89.2 1.3 %collective-permute-start.4 = (bf16[512,512]{1,0:T(8,128)(2,1)}, bf16[512,512]{1,0:T(8,128)(2,1)}, u32[]{:S(2)}, u32[]{:S(2)}) collective-permute-start(bf16[512,512]{1,0:T(8,128)(2,1)} %relay.1), channel_id=1, source_target_pairs={{1,3},{2,0},{5,7},{6,4},{9,11},{10,8},{13,15},{14,12},{17,19},{18,... | collective-permute-start | bytes 1572872 | tf_op jit(solution)/shard_map/ppermute | solution.py:351
  90.5 12.8 %all-to-all-done.2.in_ref = bf16[32,32,512]{2,1,0:T(8,128)(2,1)S(1)} async-done(((bf16[32,32,512]{2,1,0:T(8,128)(2,1)}), bf16[32,32,512]{2,1,0:T(8,128)(2,1)S(1)}, u32[]{:S(2)}, u32[]{:S(2)}) %all-to-all-start.2) | async-done | bytes 1048608 | tf_op jit(solution)/shard_map/all_to_all | solution.py:364
  103.4 0.0 copy-done
  103.4 0.0 copy-done.1
  103.4 0.0 copy-start.8
  103.4 2.4 %finish.1 = (bf16[512,512]{1,0:T(8,128)(2,1)}, bf16[512,512]{1,0:T(8,128)(2,1)}, f32[512,512]{1,0:T(8,128)}) custom-call(bf16[32,32,512]{2,1,0:T(8,128)(2,1)S(1)} %all-to-all-done.2.in_ref, bf16[512,512]{1,0:T(8,128)(2,1)S(1)} %bitcast.15, bf16[512,512]{1,0:T(8,128)(2,1)S(1)} %bitcast.13), custom_call_target="tpu_custom_call" | custom-call | flops 134217728 | bytes 2621440 | tf_op jit(solution)/shard_map/finish/pallas_call | solution.py:366
  105.8 0.0 collective-permute-done.refs_1_
  105.8 0.0 collective-permute-done.1.refs_2_
  105.8 3.7 %collective-permute-done.2.refs_3_ = bf16[512,512]{1,0:T(8,128)(2,1)} collective-permute-done((bf16[512,512]{1,0:T(8,128)(2,1)S(1)}, bf16[512,512]{1,0:T(8,128)(2,1)}, u32[]{:S(2)}, u32[]{:S(2)}) %collective-permute-start.2) | collective-permute-done | bytes 524320 | tf_op jit(solution)/shard_map/ppermute | solution.py:349
  109.5 1.9 %collective-permute-done.4.refs_4_ = bf16[512,512]{1,0:T(8,128)(2,1)} collective-permute-done((bf16[512,512]{1,0:T(8,128)(2,1)}, bf16[512,512]{1,0:T(8,128)(2,1)}, u32[]{:S(2)}, u32[]{:S(2)}) %collective-permute-start.4) | collective-permute-done | bytes 524320 | tf_op jit(solution)/shard_map/ppermute | solution.py:351
  111.5 0.0 copy-done.8
  111.5 2.6 %add_parts.1 = bf16[512,512]{1,0:T(8,128)(2,1)} custom-call(bf16[512,512]{1,0:T(8,128)(2,1)S(1)} %copy-done.8, bf16[512,512]{1,0:T(8,128)(2,1)} %collective-permute-done.refs_1_, bf16[512,512]{1,0:T(8,128)(2,1)} %collective-permute-done.1.refs_2_, bf16[512,512]{1,0:T(8,128)(2,1)} %collective-permute-done.2.refs_3_, ...), custom_call_target="tpu_custom_call" | custom-call | flops 99999997952 | bytes 3145728 | tf_op jit(solution)/shard_map/add_parts/pallas_call | solution.py:253
Async XLA Ops:
  3.9 31.6 %copy-start.5 = (bf16[896,256]{1,0:T(8,128)(2,1)S(1)}, bf16[896,256]{1,0:T(8,128)(2,1)}, u32[]{:S(2)}) copy-start(bf16[896,256]{1,0:T(8,128)(2,1)} %constant.16.clone.factors_ref) | copy-start | bytes 1376260
  3.9 31.5 %copy-start.6 = (f32[4,128,128]{2,1,0:T(8,128)S(1)}, f32[4,128,128]{2,1,0:T(8,128)}, u32[]{:S(2)}) copy-start(f32[4,128,128]{2,1,0:T(8,128)} %constant.17.clone.turn) | copy-start | bytes 786436
  35.5 22.8 %copy-start.2 = (bf16[1,512,512]{2,1,0:T(8,128)(2,1)S(1)}, bf16[1,512,512]{2,1,0:T(8,128)(2,1)}, u32[]{:S(2)}) copy-start(bf16[1,512,512]{2,1,0:T(8,128)(2,1)} %param.10) | copy-start | bytes 1572868
  35.5 22.8 %copy-start.3 = (bf16[1,512,512]{2,1,0:T(8,128)(2,1)S(1)}, bf16[1,512,512]{2,1,0:T(8,128)(2,1)}, u32[]{:S(2)}) copy-start(bf16[1,512,512]{2,1,0:T(8,128)(2,1)} %param.13) | copy-start | bytes 1572868
  41.7 0.8 copy-start.9
  42.5 15.8 %all-to-all-start.1 = ((bf16[32,16,512]{2,1,0:T(8,128)(2,1)}), bf16[32,16,512]{2,1,0:T(8,128)(2,1)S(1)}, u32[]{:S(2)}, u32[]{:S(2)}) async-start(bf16[32,16,512]{2,1,0:T(8,128)(2,1)} %get-tuple-element.16), calls=%async_computation.1 | async-start | bytes 1048576 | tf_op jit(solution)/shard_map/all_to_all | solution.py:315
  46.5 25.6 %collective-permute-start.5 = (bf16[32,16,512]{2,1,0:T(8,128)(2,1)S(1)}, bf16[32,16,512]{2,1,0:T(8,128)(2,1)}, u32[]{:S(2)}, u32[]{:S(2)}) collective-permute-start(bf16[32,16,512]{2,1,0:T(8,128)(2,1)S(1)} %get-tuple-element.22.mine_ref), channel_id=1, source_target_pairs={{0,128},{128,0},{1,129},{129,1},{2,130},{130,2},{3,131},{131,3},{4... | collective-permute-start | bytes 1572872 | tf_op jit(solution)/shard_map/ppermute | solution.py:316
  58.2 1.6 %copy-start.4 = (bf16[512,2048]{1,0:T(8,128)(2,1)S(1)}, bf16[512,2048]{1,0:T(8,128)(2,1)}, u32[]{:S(2)}) copy-start(bf16[512,2048]{1,0:T(8,128)(2,1)} %weight_ref.1) | copy-start | bytes 6291460
  59.8 12.3 %copy-start.10 = (bf16[32,16,512]{2,1,0:T(8,128)(2,1)S(1)}, bf16[32,16,512]{2,1,0:T(8,128)(2,1)}, u32[]{:S(2)}) copy-start(bf16[32,16,512]{2,1,0:T(8,128)(2,1)} %copy-done.9) | copy-start | bytes 1572868
  62.6 0.8 copy-start.7
  63.4 23.8 %collective-permute-start.3 = (bf16[512,512]{1,0:T(8,128)(2,1)}, bf16[512,512]{1,0:T(8,128)(2,1)}, u32[]{:S(2)}, u32[]{:S(2)}) collective-permute-start(bf16[512,512]{1,0:T(8,128)(2,1)} %get-tuple-element.20.refs_0_), channel_id=1, source_target_pairs={{0,1},{3,2},{4,5},{7,6},{8,9},{11,10},{12,13},{15,14},{16,17},{19,... | collective-permute-start | bytes 1572872 | tf_op jit(solution)/shard_map/ppermute | solution.py:346
  67.7 38.1 %collective-permute-start = (bf16[512,512]{1,0:T(8,128)(2,1)S(1)}, bf16[512,512]{1,0:T(8,128)(2,1)}, u32[]{:S(2)}, u32[]{:S(2)}) collective-permute-start(bf16[512,512]{1,0:T(8,128)(2,1)S(1)} %get-tuple-element.18), channel_id=1, source_target_pairs={{1,2},{2,1},{5,6},{6,5},{9,10},{10,9},{13,14},{14,13},{17,18},{18,... | collective-permute-start | bytes 1572872 | tf_op jit(solution)/shard_map/ppermute | solution.py:347
  69.2 36.6 %collective-permute-start.1 = (bf16[512,512]{1,0:T(8,128)(2,1)S(1)}, bf16[512,512]{1,0:T(8,128)(2,1)}, u32[]{:S(2)}, u32[]{:S(2)}) collective-permute-start(bf16[512,512]{1,0:T(8,128)(2,1)S(1)} %get-tuple-element.18), channel_id=1, source_target_pairs={{0,2},{3,1},{4,6},{7,5},{8,10},{11,9},{12,14},{15,13},{16,18},{19,... | collective-permute-start | bytes 1572872 | tf_op jit(solution)/shard_map/ppermute | solution.py:348
  72.1 37.4 %collective-permute-start.2 = (bf16[512,512]{1,0:T(8,128)(2,1)S(1)}, bf16[512,512]{1,0:T(8,128)(2,1)}, u32[]{:S(2)}, u32[]{:S(2)}) collective-permute-start(bf16[512,512]{1,0:T(8,128)(2,1)S(1)} %get-tuple-element.19), channel_id=1, source_target_pairs={{0,1},{3,2},{1,0},{2,3},{4,5},{7,6},{5,4},{6,7},{8,9},{11,10},{9,8... | collective-permute-start | bytes 1572872 | tf_op jit(solution)/shard_map/ppermute | solution.py:349
  74.3 29.1 %all-to-all-start.2 = ((bf16[32,32,512]{2,1,0:T(8,128)(2,1)}), bf16[32,32,512]{2,1,0:T(8,128)(2,1)S(1)}, u32[]{:S(2)}, u32[]{:S(2)}) async-start(bf16[32,32,512]{2,1,0:T(8,128)(2,1)} %join.1), calls=%async_computation.2 | async-start | bytes 2097152 | tf_op jit(solution)/shard_map/all_to_all | solution.py:364
  86.2 17.2 %copy-start = (bf16[1,512,512]{2,1,0:T(8,128)(2,1)S(1)}, bf16[1,512,512]{2,1,0:T(8,128)(2,1)}, u32[]{:S(2)}) copy-start(bf16[1,512,512]{2,1,0:T(8,128)(2,1)} %param.8) | copy-start | bytes 1572868
  86.2 17.2 %copy-start.1 = (bf16[1,512,512]{2,1,0:T(8,128)(2,1)S(1)}, bf16[1,512,512]{2,1,0:T(8,128)(2,1)}, u32[]{:S(2)}) copy-start(bf16[1,512,512]{2,1,0:T(8,128)(2,1)} %param.9) | copy-start | bytes 1572868
  89.2 22.3 %collective-permute-start.4 = (bf16[512,512]{1,0:T(8,128)(2,1)}, bf16[512,512]{1,0:T(8,128)(2,1)}, u32[]{:S(2)}, u32[]{:S(2)}) collective-permute-start(bf16[512,512]{1,0:T(8,128)(2,1)} %relay.1), channel_id=1, source_target_pairs={{1,3},{2,0},{5,7},{6,4},{9,11},{10,8},{13,15},{14,12},{17,19},{18,... | collective-permute-start | bytes 1572872 | tf_op jit(solution)/shard_map/ppermute | solution.py:351
  103.4 8.1 %copy-start.8 = (bf16[512,512]{1,0:T(8,128)(2,1)S(1)}, bf16[512,512]{1,0:T(8,128)(2,1)}, u32[]{:S(2)}) copy-start(bf16[512,512]{1,0:T(8,128)(2,1)} %copy-done.7) | copy-start | bytes 1572868
